TPU v7x, 128 devices: a whole 4x4x4 slice. The times are simulated.
128 devices in a mesh: dp: 32 (over z, y, core), blk: 4 (over x).
Axes of the slice: x: 4, y: 4, z: 4, core: 2. Of those that a mesh axis runs over, the one named last changes fastest.
Arguments:
- queries: bfloat16 [16384, 4096], P(('dp', 'blk')), may hold values from -24 to 24
- passages: bfloat16 [98304, 4096], P(('dp', 'blk')), may hold values from -6 to 6
- neg_table: bfloat16 [32768, 4096], P('dp'), may hold values from -6 to 6
- neg_ids: int32 [16384, 16], P(('dp', 'blk')), may hold values from 0 to 32767, as said below
- counts: int32 [16384], P(('dp', 'blk')), may hold values from 1 to 16
- neg_home: int32 [32768], replicated, may hold values from 0 to 32767, as said below
Outputs:
- loss: float32 [16384], P(('dp', 'blk'))
- grad_queries: bfloat16 [16384, 4096], P(('dp', 'blk'))
- grad_passages: bfloat16 [98304, 4096], P(('dp', 'blk'))
Inputs may be any that keep to these rules, and one draw needn't show every extreme that they name: `neg_ids`: within each device's 128 queries, the slots (query, k) taken in order in groups of 64 name passages held by one index of dp each, a different index for each group. `neg_home`: each index row is named once.
All inputs are finite; a program needn't handle non-finite values.
Results may differ from a plain program's by a relative error of at most 0.0065.
Values may be sent and summed in bfloat16 or wider, within the bound.
A program may use at most 192 MiB of HBM per device.

v0:
```python
import jax
import jax.numpy as jnp
from jax import lax
from jax.sharding import PartitionSpec as P

score_scale = 0.0625


def from_behind(block, axis, distance):
    devices = range(lax.axis_size(axis))
    route = [((i - distance) % len(devices), i) for i in devices]
    return lax.ppermute(block, axis, route)


def fetch_negatives(neg_ids, neg_home, neg_table):
    per_dev, slots = neg_ids.shape
    owner_count = lax.axis_size("dp")
    share = neg_table.shape[0]
    width = per_dev * slots // owner_count
    rows = neg_home[neg_ids.reshape(-1)]
    owners = (rows // share).reshape(owner_count, width)
    places = (rows % share).reshape(owner_count, width)
    block_owner = owners[:, 0]
    order = (
        jnp.zeros((owner_count,), jnp.int32)
        .at[block_owner]
        .set(jnp.arange(owner_count, dtype=jnp.int32))
    )
    request = places[order]
    found = neg_table[lax.all_to_all(request, "dp", split_axis=0, concat_axis=0, tiled=True)]
    fetched = lax.all_to_all(found, "dp", split_axis=0, concat_axis=0, tiled=True)
    return fetched[block_owner].reshape(per_dev, slots, neg_table.shape[1])


def fold_scores(stats, scores):
    top = jnp.maximum(stats[0], jnp.max(scores, 1))
    total = stats[1] * jnp.exp(stats[0] - top) + jnp.sum(jnp.exp(scores - top[:, None]), 1)
    return jnp.stack([top, total])


def rotate_block(block):
    return from_behind(block, "blk", 1)


def rotate_sums(values):
    return from_behind(values, "blk", 1)


def score_block(block, passages):
    return score_scale * jnp.dot(block, passages.T, preferred_element_type=jnp.float32)


def per_device(queries, passages, neg_table, neg_ids, counts, neg_home):
    per_dev = queries.shape[0]
    group_len = lax.axis_size("blk")
    me = lax.axis_index("blk")
    slots = neg_ids.shape[1]
    negatives = fetch_negatives(neg_ids, neg_home, neg_table)
    neg_scores = score_scale * jnp.einsum(
        "qd,qkd->qk", queries, negatives, preferred_element_type=jnp.float32
    )
    live = jnp.arange(slots, dtype=jnp.int32)[None, :] < counts[:, None]
    neg_top = jnp.max(jnp.where(live, neg_scores, -jnp.inf), 1)
    neg_total = jnp.sum(
        jnp.where(live, jnp.exp(neg_scores - neg_top[:, None]), jnp.float32(0.0)), 1
    )
    positive = passages[:per_dev]
    pos_score = score_scale * jnp.sum(queries.astype(jnp.float32) * positive.astype(jnp.float32), 1)
    block = queries
    stats = jnp.stack([neg_top, neg_total])
    kept_blocks = []
    kept_scores = []
    for step in range(group_len):
        tile = score_block(block, passages)
        kept_blocks.append(block)
        kept_scores.append(tile)
        stats = fold_scores(stats, tile)
        if step + 1 < group_len:
            block = rotate_block(block)
        stats = rotate_sums(stats)
    lse = stats[0] + jnp.log(stats[1])
    lse_all = lax.all_gather(lse, "blk", axis=0, tiled=True)
    neg_weights = jnp.where(live, jnp.exp(neg_scores - lse[:, None]), jnp.float32(0.0)).astype(
        jnp.bfloat16
    )
    summed = score_scale * (
        jnp.einsum("qk,qkd->qd", neg_weights, negatives, preferred_element_type=jnp.float32)
        - positive.astype(jnp.float32)
    )
    grad_p = jnp.zeros((passages.shape[0], passages.shape[1]), jnp.float32)
    for step in range(group_len):
        anchor = (me - step) % group_len
        lse_block = lax.dynamic_slice_in_dim(lse_all, anchor * per_dev, per_dev)
        weights = jnp.exp(kept_scores[step] - lse_block[:, None]).astype(jnp.bfloat16)
        summed = summed + score_scale * jnp.dot(
            weights, passages, preferred_element_type=jnp.float32
        )
        grad_p = grad_p + score_scale * lax.dot_general(
            weights, kept_blocks[step], (((0,), (0,)), ((), ())), preferred_element_type=jnp.float32
        )
        summed = rotate_sums(summed)
    loss = lse - pos_score
    grad_p = grad_p.at[:per_dev].add(-score_scale * queries.astype(jnp.float32))
    return (loss, summed.astype(jnp.bfloat16), grad_p.astype(jnp.bfloat16))


def solution(mesh):
    in_specs = (
        P(("dp", "blk"), None),
        P(("dp", "blk"), None),
        P("dp", None),
        P(("dp", "blk"), None),
        P(("dp", "blk")),
        P(),
    )
    out_specs = (P(("dp", "blk")), P(("dp", "blk"), None), P(("dp", "blk"), None))
    return jax.shard_map(
        per_device, mesh=mesh, in_specs=in_specs, out_specs=out_specs, check_vma=False
    )
```

profile of v0, /device:TPU:0, one launch (start us, length us, event | category | flops | bytes accessed | tf_op | source)
XLA Modules:
  0.0 522.1 jit_solution(16177273840830056749)
XLA Ops:
  0.6 0.0 copy-start
  0.6 0.8 copy.12
  1.5 0.1 reshape.192
  1.6 11.8 %gather_fusion = s32[2048]{0:T(1024)S(1)} fusion(s32[32768]{0:T(1024)S(1)} %copy-done, s32[2048]{0:T(1024)S(1)} %broadcast_clamp_fusion.1), kind=kCustom, calls=%fused_computation | custom fusion | bytes 24576 | tf_op jit(solution)/shard_map/gather | solution.py:20
  13.4 0.1 gather.15
  13.5 0.1 fusion.7
  13.6 0.7 scatter_custom_fusion
  14.3 0.6 gather_fusion.1
  14.9 15.6 %all_to_all.17 = s32[32,1,64]{2,1,0:T(1,128)S(1)} all-to-all(s32[32,1,64]{2,1,0:T(1,128)S(1)} %bitcast.102), channel_id=1, replica_groups=mesh['dp'=32,'blk'=4] {'dp'}, dimensions={0} | all-to-all | bytes 16384 | tf_op jit(solution)/shard_map/all_to_all | solution.py:30
  30.5 0.1 reshape.212
  30.6 33.1 %gather_fusion.2 = bf16[2048,4096]{1,0:T(8,128)(2,1)} fusion(bf16[1024,4096]{1,0:T(8,128)(2,1)} %param.10, s32[2048]{0:T(1024)S(1)} %broadcast_clamp_fusion), kind=kCustom, calls=%fused_computation.2 | custom fusion | bytes 33562624 | tf_op jit(solution)/shard_map/gather | solution.py:30
  63.7 5.3 %all-to-all-start.1 = ((bf16[32,64,4096]{2,1,0:T(8,128)(2,1)}), bf16[32,64,4096]{2,1,0:T(8,128)(2,1)}, u32[]{:S(2)}, u32[]{:S(2)}) async-start(bf16[32,64,4096]{2,1,0:T(8,128)(2,1)} %bitcast.100), calls=%async_computation.1 | async-start | bytes 33554432 | tf_op jit(solution)/shard_map/all_to_all | solution.py:31
  69.0 1.6 collective-permute-start.1
  70.6 1.6 fusion.4
  72.2 5.1 fusion.25
  77.2 18.2 %collective-permute-done.1 = bf16[128,4096]{1,0:T(8,128)(2,1)S(1)} collective-permute-done((bf16[128,4096]{1,0:T(8,128)(2,1)S(1)}, bf16[128,4096]{1,0:T(8,128)(2,1)S(1)}, u32[]{:S(2)}, u32[]{:S(2)}) %collective-permute-start.1) | collective-permute-done | bytes 1048608 | tf_op jit(solution)/shard_map/ppermute | solution.py:12
  95.4 0.3 collective-permute-start.3
  95.7 186.5 %all-to-all-done.1 = bf16[32,64,4096]{2,1,0:T(8,128)(2,1)} async-done(((bf16[32,64,4096]{2,1,0:T(8,128)(2,1)}), bf16[32,64,4096]{2,1,0:T(8,128)(2,1)}, u32[]{:S(2)}, u32[]{:S(2)}) %all-to-all-start.1) | async-done | bytes 16777248 | tf_op jit(solution)/shard_map/all_to_all | solution.py:31
  282.2 13.1 %gather_fusion.3 = bf16[32,64,4096]{2,1,0:T(8,128)(2,1)} fusion(bf16[32,64,4096]{2,1,0:T(8,128)(2,1)} %all-to-all-done.1, s32[1024]{0:T(1024)S(1)} %pad_clamp_fusion), kind=kCustom, calls=%fused_computation.3 | custom fusion | bytes 33554560 | tf_op jit(solution)/shard_map/gather | solution.py:32
  295.3 9.2 %fusion.5 = f32[128,1,16]{2,1,0:T(1,128)S(1)} fusion(bf16[128,16,4096]{2,1,0:T(8,128)(2,1)} %bitcast.98, bf16[128,4096,1]{1,0,2:T(8,128)(2,1)S(1)} %bitcast.101), kind=kOutput, calls=%fused_computation.18 | convolution fusion | flops 16777216 | bytes 17833984 | tf_op jit(solution)/shard_map/qd,qkd->qk/dot_general | solution.py:59
  304.7 0.2 exponential_reduce_fusion.3
  304.9 0.0 slice-start
  304.9 1.7 collective-permute-start
  306.7 5.1 fusion.24
  311.8 1.6 collective-permute-start.5
  313.3 0.2 exponential_reduce_fusion.2
  313.6 0.0 slice-start.1
  313.6 1.3 collective-permute-start.2
  314.9 5.4 %fusion.23 = (f32[128]{0:T(128)S(1)}, f32[128,768]{1,0:T(8,128)S(1)}) fusion(bf16[128,4096]{1,0:T(8,128)(2,1)} %collective-permute-done.3, bf16[768,4096]{1,0:T(8,128)(2,1)} %param.9), kind=kOutput, calls=%fused_computation.92 | convolution fusion | flops 805502848 | bytes 7733760 | tf_op jit(solution)/shard_map/dot_general | solution.py:50
  320.3 7.8 %collective-permute-done.2 = f32[2,128]{1,0:T(2,128)S(1)} collective-permute-done((f32[2,128]{1,0:T(2,128)S(1)}, f32[2,128]{1,0:T(2,128)S(1)}, u32[]{:S(2)}, u32[]{:S(2)}) %collective-permute-start.2) | collective-permute-done | bytes 1056 | tf_op jit(solution)/shard_map/ppermute | solution.py:12
  328.1 0.2 exponential_reduce_fusion.1
  328.4 0.4 collective-permute-start.4
  328.8 0.0 slice-start.2
  328.8 2.3 fusion.22
  331.1 2.1 collective-permute-done.4
  333.2 0.2 exponential_reduce_fusion
  333.5 0.1 collective-permute-start.6
  333.6 4.7 collective-permute-done.6
  338.3 0.5 multiply_subtract_fusion
  338.9 7.2 %all-gather = f32[1,512]{1,0:T(1,128)S(1)} all-gather(f32[1,128]{1,0:T(1,128)S(1)} %get-tuple-element.16), channel_id=2, replica_groups=mesh['dp'=32,'blk'=4] {'blk'}, dimensions={1}, use_global_device_ids=true | all-gather | bytes 2560 | tf_op jit(solution)/shard_map/all_gather | solution.py:82
  346.1 0.1 copy.16
  346.2 0.0 slice-start.3
  346.3 8.6 %fusion.26 = f32[128,1,4096]{2,1,0:T(1,128)S(1)} fusion(bf16[128,16,1]{1,2,0:T(2,128)(2,1)S(1)} %copy.16, bf16[128,16,4096]{2,1,0:T(8,128)(2,1)} %bitcast.99), kind=kOutput, calls=%fused_computation.95 | convolution fusion | flops 16777216 | bytes 18878464 | tf_op jit(solution)/shard_map/qk,qkd->qd/dot_general | solution.py:87
  354.9 2.5 fusion.1
  357.4 2.0 collective-permute-start.7
  359.4 42.7 %collective-permute-done.7 = f32[128,4096]{1,0:T(8,128)S(1)} collective-permute-done((f32[128,4096]{1,0:T(8,128)S(1)}, f32[128,4096]{1,0:T(8,128)S(1)}, u32[]{:S(2)}, u32[]{:S(2)}) %collective-permute-start.7) | collective-permute-done | bytes 2097184 | tf_op jit(solution)/shard_map/ppermute | solution.py:12
  402.1 1.3 fusion
  403.4 0.9 collective-permute-start.8
  404.3 1.1 convolution_multiply_fusion.1
  405.4 43.5 %collective-permute-done.8 = f32[128,4096]{1,0:T(8,128)S(1)} collective-permute-done((f32[128,4096]{1,0:T(8,128)S(1)}, f32[128,4096]{1,0:T(8,128)S(1)}, u32[]{:S(2)}, u32[]{:S(2)}) %collective-permute-start.8) | collective-permute-done | bytes 2097184 | tf_op jit(solution)/shard_map/ppermute | solution.py:12
  448.9 0.3 add.156
  449.2 0.9 collective-permute-start.9
  450.1 1.1 convolution_multiply_fusion
  451.2 0.0 copy-start.13
  451.2 6.4 %fusion.19 = f32[768,4096]{1,0:T(8,128)} fusion(bf16[128,4096]{1,0:T(8,128)(2,1)S(1)} %copy-done.2, f32[128,768]{1,0:T(8,128)S(1)} %copy-done.11, f32[128]{0:T(128)S(1)} %get-tuple-element.30), kind=kOutput, calls=%fused_computation.88 | convolution fusion | flops 805502976 | bytes 14025216 | tf_op jit(solution)/shard_map/dot_general | solution.py:98
  457.6 6.5 %fusion.20 = f32[768,4096]{1,0:T(8,128)} fusion(bf16[128,4096]{1,0:T(8,128)(2,1)S(1)} %copy-done.13, f32[128,768]{1,0:T(8,128)S(1)} %copy-done.4, f32[128]{0:T(128)S(1)} %get-tuple-element.29), kind=kOutput, calls=%fused_computation.89 | convolution fusion | flops 805502976 | bytes 14025216 | tf_op jit(solution)/shard_map/dot_general | solution.py:98
  464.1 7.8 %fusion.21 = f32[768,4096]{1,0:T(8,128)} fusion(bf16[128,4096]{1,0:T(8,128)(2,1)} %collective-permute-done.3, f32[128,768]{1,0:T(8,128)S(1)} %copy-done.9, f32[128]{0:T(128)S(1)} %get-tuple-element.28), kind=kOutput, calls=%fused_computation.90 | convolution fusion | flops 805502976 | bytes 14025216 | tf_op jit(solution)/shard_map/dot_general | solution.py:98
  471.9 19.5 %collective-permute-done.9 = f32[128,4096]{1,0:T(8,128)S(1)} collective-permute-done((f32[128,4096]{1,0:T(8,128)S(1)}, f32[128,4096]{1,0:T(8,128)S(1)}, u32[]{:S(2)}, u32[]{:S(2)}) %collective-permute-start.9) | collective-permute-done | bytes 2097184 | tf_op jit(solution)/shard_map/ppermute | solution.py:12
  491.4 0.2 add.159
  491.6 0.1 collective-permute-start.10
  491.7 18.0 %add_multiply_fusion = f32[768,4096]{1,0:T(8,128)} fusion(f32[768,4096]{1,0:T(8,128)} %fusion.21, f32[768,4096]{1,0:T(8,128)} %fusion.19, f32[768,4096]{1,0:T(8,128)} %fusion.20, bf16[128,4096]{1,0:T(8,128)(2,1)S(1)} %copy-done.15, f32[128,768]{1,0:T(8,128)S(1)} %copy-done.7, f32[128]{0:T(128)S(1)} %get-tuple-element.27), kind=kOutput, calls=%fused_computation.5 | convolution fusion | flops 818085888 | bytes 51773952 | tf_op jit(solution)/shard_map/dot_general | solution.py:98
  509.7 3.2 fusion.3
  512.9 8.2 %convert_element_type.37 = bf16[768,4096]{1,0:T(8,128)(2,1)} convert(f32[768,4096]{1,0:T(8,128)} %fusion.3) | non-fusion elementwise | flops 3145728 | bytes 18874368 | tf_op jit(solution)/shard_map/convert_element_type | solution.py:104
  521.1 1.0 copy.23
  (69 shorter events, 0.4 us)
Async XLA Ops:
  0.6 1.0 copy-start
  63.7 5.3 %copy-start.2 = (bf16[128,4096]{1,0:T(8,128)(2,1)S(1)}, bf16[128,4096]{1,0:T(8,128)(2,1)}, u32[]{:S(2)}) copy-start(bf16[128,4096]{1,0:T(8,128)(2,1)} %param.8) | copy-start | bytes 3145732
  63.7 218.6 %all-to-all-start.1 = ((bf16[32,64,4096]{2,1,0:T(8,128)(2,1)}), bf16[32,64,4096]{2,1,0:T(8,128)(2,1)}, u32[]{:S(2)}, u32[]{:S(2)}) async-start(bf16[32,64,4096]{2,1,0:T(8,128)(2,1)} %bitcast.100), calls=%async_computation.1 | async-start | bytes 33554432 | tf_op jit(solution)/shard_map/all_to_all | solution.py:31
  69.0 26.4 %collective-permute-start.1 = (bf16[128,4096]{1,0:T(8,128)(2,1)S(1)}, bf16[128,4096]{1,0:T(8,128)(2,1)S(1)}, u32[]{:S(2)}, u32[]{:S(2)}) collective-permute-start(bf16[128,4096]{1,0:T(8,128)(2,1)S(1)} %copy-done.2), channel_id=1, source_target_pairs={{3,0},{0,1},{1,2},{2,3},{7,4},{4,5},{5,6},{6,7},{11,8},{8,9},{9,10... | collective-permute-start | bytes 3145736 | tf_op jit(solution)/shard_map/ppermute | solution.py:12
  77.2 227.4 %copy-start.10 = (f32[128,768]{1,0:T(8,128)}, f32[128,768]{1,0:T(8,128)S(1)}, u32[]{:S(2)}) copy-start(f32[128,768]{1,0:T(8,128)S(1)} %get-tuple-element.40) | copy-start | bytes 1179652
  95.4 211.2 %copy-start.12 = (bf16[128,4096]{1,0:T(8,128)(2,1)}, bf16[128,4096]{1,0:T(8,128)(2,1)S(1)}, u32[]{:S(2)}) copy-start(bf16[128,4096]{1,0:T(8,128)(2,1)S(1)} %collective-permute-done.1) | copy-start | bytes 3145732
  95.4 216.3 %collective-permute-start.3 = (bf16[128,4096]{1,0:T(8,128)(2,1)S(1)}, bf16[128,4096]{1,0:T(8,128)(2,1)}, u32[]{:S(2)}, u32[]{:S(2)}) collective-permute-start(bf16[128,4096]{1,0:T(8,128)(2,1)S(1)} %collective-permute-done.1), channel_id=1, source_target_pairs={{3,0},{0,1},{1,2},{2,3},{7,4},{4,5},{5,6},{6,7},{11,8},{8,9},{9,10... | collective-permute-start | bytes 3145736 | tf_op jit(solution)/shard_map/ppermute | solution.py:12
  295.3 9.3 %copy-start.16 = (s32[128]{0:T(128)S(1)}, s32[128]{0:T(128)}, u32[]{:S(2)}) copy-start(s32[128]{0:T(128)} %param.12) | copy-start | bytes 1540
  304.9 23.8 %slice-start = ((s8[6291456]{0:T(1024)(128)(4,1)}), s8[4194304]{0:T(1024)(128)(4,1)S(1)}, s32[]{:S(2)}) async-start(s8[6291456]{0:T(1024)(128)(4,1)} %bitcast.94), calls=%async_computation.2 | async-start | bytes 8388608
  304.9 8.4 %collective-permute-start = (f32[2,128]{1,0:T(2,128)S(1)}, f32[2,128]{1,0:T(2,128)S(1)}, u32[]{:S(2)}, u32[]{:S(2)}) collective-permute-start(f32[2,128]{1,0:T(2,128)S(1)} %pad_maximum_fusion), channel_id=1, source_target_pairs={{3,0},{0,1},{1,2},{2,3},{7,4},{4,5},{5,6},{6,7},{11,8},{8,9},{9,10... | collective-permute-start | bytes 3080 | tf_op jit(solution)/shard_map/ppermute | solution.py:12
  311.8 1.6 copy-start.3
  311.8 17.0 %collective-permute-start.5 = (bf16[128,4096]{1,0:T(8,128)(2,1)}, bf16[128,4096]{1,0:T(8,128)(2,1)S(1)}, u32[]{:S(2)}, u32[]{:S(2)}) collective-permute-start(bf16[128,4096]{1,0:T(8,128)(2,1)} %collective-permute-done.3), channel_id=1, source_target_pairs={{3,0},{0,1},{1,2},{2,3},{7,4},{4,5},{5,6},{6,7},{11,8},{8,9},{9,10... | collective-permute-start | bytes 3145736 | tf_op jit(solution)/shard_map/ppermute | solution.py:12
  313.6 15.2 %slice-start.1 = ((s8[6291456]{0:T(1024)(128)(4,1)}), s8[2097152]{0:T(1024)(128)(4,1)S(1)}, s32[]{:S(2)}) async-start(s8[6291456]{0:T(1024)(128)(4,1)} %bitcast.94), calls=%async_computation.3 | async-start | bytes 4194304
  313.6 14.5 %collective-permute-start.2 = (f32[2,128]{1,0:T(2,128)S(1)}, f32[2,128]{1,0:T(2,128)S(1)}, u32[]{:S(2)}, u32[]{:S(2)}) collective-permute-start(f32[2,128]{1,0:T(2,128)S(1)} %pad_maximum_fusion.1), channel_id=1, source_target_pairs={{3,0},{0,1},{1,2},{2,3},{7,4},{4,5},{5,6},{6,7},{11,8},{8,9},{9,10... | collective-permute-start | bytes 3080 | tf_op jit(solution)/shard_map/ppermute | solution.py:12
  320.3 8.5 %copy-start.8 = (f32[128,768]{1,0:T(8,128)}, f32[128,768]{1,0:T(8,128)S(1)}, u32[]{:S(2)}) copy-start(f32[128,768]{1,0:T(8,128)S(1)} %get-tuple-element.36) | copy-start | bytes 1179652
  328.4 4.8 collective-permute-start.4
  328.8 4.7 copy-start.14
  328.8 26.1 %slice-start.2 = ((s8[6291456]{0:T(1024)(128)(4,1)}), s8[2097152]{0:T(1024)(128)(4,1)S(1)}, s32[]{:S(2)}) async-start(s8[6291456]{0:T(1024)(128)(4,1)} %bitcast.96), calls=%async_computation.4 | async-start | bytes 4194304
  331.1 2.2 copy-start.5
  333.5 4.8 collective-permute-start.6
  346.2 8.6 %slice-start.3 = ((s8[6291456]{0:T(1024)(128)(4,1)}), s8[4194304]{0:T(1024)(128)(4,1)S(1)}, s32[]{:S(2)}) async-start(s8[6291456]{0:T(1024)(128)(4,1)} %bitcast.96), calls=%async_computation.5 | async-start | bytes 8388608
  346.3 8.6 %copy-start.11 = (f32[128,768]{1,0:T(8,128)S(1)}, f32[128,768]{1,0:T(8,128)}, u32[]{:S(2)}) copy-start(f32[128,768]{1,0:T(8,128)} %copy-done.10) | copy-start | bytes 1179652
  354.9 47.2 %copy-start.4 = (f32[128,768]{1,0:T(8,128)S(1)}, f32[128,768]{1,0:T(8,128)}, u32[]{:S(2)}) copy-start(f32[128,768]{1,0:T(8,128)} %copy-done.3) | copy-start | bytes 1179652
  357.4 44.7 %collective-permute-start.7 = (f32[128,4096]{1,0:T(8,128)S(1)}, f32[128,4096]{1,0:T(8,128)S(1)}, u32[]{:S(2)}, u32[]{:S(2)}) collective-permute-start(f32[128,4096]{1,0:T(8,128)S(1)} %fusion.1), channel_id=1, source_target_pairs={{3,0},{0,1},{1,2},{2,3},{7,4},{4,5},{5,6},{6,7},{11,8},{8,9},{9,10... | collective-permute-start | bytes 6291464 | tf_op jit(solution)/shard_map/ppermute | solution.py:12
  402.1 2.2 copy-start.9
  403.4 45.5 %collective-permute-start.8 = (f32[128,4096]{1,0:T(8,128)S(1)}, f32[128,4096]{1,0:T(8,128)S(1)}, u32[]{:S(2)}, u32[]{:S(2)}) collective-permute-start(f32[128,4096]{1,0:T(8,128)S(1)} %fusion), channel_id=1, source_target_pairs={{3,0},{0,1},{1,2},{2,3},{7,4},{4,5},{5,6},{6,7},{11,8},{8,9},{9,10... | collective-permute-start | bytes 6291464 | tf_op jit(solution)/shard_map/ppermute | solution.py:12
  405.4 44.7 %copy-start.6 = (f32[128,768]{1,0:T(8,128)S(1)}, f32[128,768]{1,0:T(8,128)}, u32[]{:S(2)}) copy-start(f32[128,768]{1,0:T(8,128)} %copy-done.5) | copy-start | bytes 1179652
  449.2 42.2 %collective-permute-start.9 = (f32[128,4096]{1,0:T(8,128)S(1)}, f32[128,4096]{1,0:T(8,128)S(1)}, u32[]{:S(2)}, u32[]{:S(2)}) collective-permute-start(f32[128,4096]{1,0:T(8,128)S(1)} %add.156), channel_id=1, source_target_pairs={{3,0},{0,1},{1,2},{2,3},{7,4},{4,5},{5,6},{6,7},{11,8},{8,9},{9,10... | collective-permute-start | bytes 6291464 | tf_op jit(solution)/shard_map/ppermute | solution.py:12
  451.2 6.4 %copy-start.13 = (bf16[128,4096]{1,0:T(8,128)(2,1)S(1)}, bf16[128,4096]{1,0:T(8,128)(2,1)}, u32[]{:S(2)}) copy-start(bf16[128,4096]{1,0:T(8,128)(2,1)} %copy-done.12) | copy-start | bytes 3145732
  464.1 27.5 %copy-start.7 = (f32[128,768]{1,0:T(8,128)S(1)}, f32[128,768]{1,0:T(8,128)}, u32[]{:S(2)}) copy-start(f32[128,768]{1,0:T(8,128)} %copy-done.5) | copy-start | bytes 1179652
  464.1 27.6 %copy-start.15 = (bf16[128,4096]{1,0:T(8,128)(2,1)S(1)}, bf16[128,4096]{1,0:T(8,128)(2,1)}, u32[]{:S(2)}) copy-start(bf16[128,4096]{1,0:T(8,128)(2,1)} %copy-done.14) | copy-start | bytes 3145732
  491.6 29.6 %collective-permute-start.10 = (bf16[128,4096]{1,0:T(8,128)(2,1)S(1)}, bf16[128,4096]{1,0:T(8,128)(2,1)S(1)}, u32[]{:S(2)}, u32[]{:S(2)}) collective-permute-start(bf16[128,4096]{1,0:T(8,128)(2,1)S(1)} %add.159), channel_id=1, source_target_pairs={{3,0},{0,1},{1,2},{2,3},{7,4},{4,5},{5,6},{6,7},{11,8},{8,9},{9,10... | collective-permute-start | bytes 3145736 | tf_op jit(solution)/shard_map/ppermute | solution.py:12
  509.7 12.4 %copy-start.1 = (s32[32768]{0:T(1024)S(1)}, s32[32768]{0:T(1024)}, u32[]{:S(2)}) copy-start(s32[32768]{0:T(1024)} %param.13) | copy-start | bytes 393220
where the time goes:
time: 530 us; the launch traced here: 522 us
  waiting for transfers between devices  325 us (61%)
  matrix products  80.2 us (15%)
  local copies, waits for them, and re-layouts  61.5 us (12%)
  blocking collectives  22.8 us (4%)
  starting transfers between devices  16.1 us (3%)
  other arithmetic  15.2 us (3%)
    all_to_all x1, waiting for transfers between devices, fetch_negatives(): lax.all_to_all(found, 'dp', split_axis=0, concat_axis=0, tiled=True)  187 us
    ppermute x11, waiting for transfers between devices, from_behind(): return lax.ppermute(block, axis, route)  139 us
    dot_general x4, matrix products, per_device(): lax.dot_general(weights, kept_blocks[step], (((0,), (0,)), ((), ())), pre...  38.7 us
    gather x1, local copies, waits for them, and re-layouts, fetch_negatives(): neg_table[lax.all_to_all(request, 'dp', split_axis=0, concat_axis=0, tile...  33.1 us
    dot_general x4, matrix products, score_block(): jnp.dot(block, passages.T, preferred_element_type=jnp.float32)  17.9 us
    all_to_all x1, blocking collectives, fetch_negatives(): lax.all_to_all(request, 'dp', split_axis=0, concat_axis=0, tiled=True)  15.6 us
    gather x1, local copies, waits for them, and re-layouts, fetch_negatives(): return fetched[block_owner].reshape(per_dev, slots, neg_table.shape[1])  13.1 us
    gather x2, local copies, waits for them, and re-layouts, fetch_negatives(): rows = neg_home[neg_ids.reshape(-1)]  11.9 us
  transfers between devices with their start and end apart: 12, of which 8 were waited for; matrix products, arithmetic and copies ran while one was open for 18% of the time, Pallas kernels for 0%

commit v1 on v0

v1 whole, which is shorter than its diff:
```python
import functools

import jax
import jax.numpy as jnp
from jax import lax
from jax.experimental import pallas as pl
from jax.experimental.pallas import tpu as pltpu
from jax.sharding import PartitionSpec as P

MESH = pl.DeviceIdType.MESH
F32, BF16, I32 = jnp.float32, jnp.bfloat16, jnp.int32
SCALE = 0.0625
META = 128
PIECES = 4
SUBS = 2


def nn(a, b):
    return jnp.dot(a, b, preferred_element_type=F32)


def nt(a, b):
    return lax.dot_general(a, b, (((1,), (1,)), ((), ())), preferred_element_type=F32)


def tn(a, b):
    return lax.dot_general(a, b, (((0,), (0,)), ((), ())), preferred_element_type=F32)


def iota(shape, dim):
    return lax.broadcasted_iota(I32, shape, dim)


def to_row(col):
    n = col.shape[0]
    eye = iota((n, n), 0) == iota((n, n), 1)
    return jnp.sum(jnp.where(eye, col, jnp.zeros_like(col)), 0, keepdims=True)


def to_col(row):
    n = row.shape[1]
    eye = iota((n, n), 0) == iota((n, n), 1)
    return jnp.sum(jnp.where(eye, row, jnp.zeros_like(row)), 1, keepdims=True)


def one_hot(cond):
    return jnp.where(cond, 1.0, 0.0).astype(BF16)


def loop(n, body):
    lax.fori_loop(0, n, lambda t, carry: (body(t), carry)[1], 0)


def exchange_kernel(
    n_dp, q_hbm, p_hbm, t_hbm, ids_ref, counts_ref, home_ref,
    qall_hbm, w_ref, gq_ref, loss_ref,
    qv, pv, tv, s_ref, e_ref, mcol, lcol, ob, base, arecv, grecv,
    req_out, req_in, ret_out, ret_in, qr, sneg, eneg, oneg,
    st_out, st_in, lse_out, lse_in,
    local_sem, out_sem, ag_s, ag_r, rs_s, rs_r, st_s, st_r, ls_s, ls_r,
    rq_s, rq_r, rt_s, rt_r,
):
    qd, d = q_hbm.shape
    pd = p_hbm.shape[0]
    half, piece = qd // 2, d // PIECES
    sub = half // SUBS
    slots = ids_ref.shape[1]
    nx = 4
    dp, me = lax.axis_index("dp"), lax.axis_index("blk")
    right = (dp, lax.rem(me + 1, nx))
    left = (dp, lax.rem(me + nx - 1, nx))
    across = (dp, lax.rem(me + 2, nx))

    barrier = pltpu.get_barrier_semaphore()
    for peer in (right, left, across):
        pl.semaphore_signal(barrier, inc=1, device_id=peer, device_id_type=MESH)

    def greet(j):
        peer = lax.rem(dp + j + 1, n_dp)
        pl.semaphore_signal(barrier, inc=1, device_id=(peer, me), device_id_type=MESH)

    loop(n_dp - 1, greet)
    q_in = pltpu.make_async_copy(q_hbm, qv.at[pl.ds(0, qd)], local_sem.at[0])
    p_in = pltpu.make_async_copy(p_hbm, pv, local_sem.at[1])
    t_in = pltpu.make_async_copy(t_hbm, tv, local_sem.at[2])
    q_in.start()
    p_in.start()
    t_in.start()
    pl.semaphore_wait(barrier, n_dp + 2)

    def remote(src, dst, send, recv, peer):
        return pltpu.make_async_remote_copy(
            src_ref=src, dst_ref=dst, send_sem=send, recv_sem=recv, device_id=peer, device_id_type=MESH
        )

    def rows(slot, part):
        return pl.ds(slot * qd + part * half, half)

    def gather_step(i, src, slot, part, peer):
        return remote(src, qv.at[rows(slot, part)], ag_s.at[i], ag_r.at[i], peer)

    own = [q_hbm.at[pl.ds(0, half)], q_hbm.at[pl.ds(half, half)]]
    ag_r1 = gather_step(0, own[0], 1, 0, right)
    ag_l1 = gather_step(1, own[1], 2, 1, left)
    ag_r2 = gather_step(2, own[1], 1, 1, right)
    ag_l2 = gather_step(3, own[0], 2, 0, left)
    ag_r3 = gather_step(4, qv.at[rows(1, 0)], 3, 0, right)
    ag_l3 = gather_step(5, qv.at[rows(2, 1)], 3, 1, left)
    for copy in (ag_r1, ag_l1, ag_r2, ag_l2):
        copy.start()

    n_msg = n_dp * 16
    ids = ids_ref[...]
    home = home_ref[...]
    live = iota((qd, slots), 1) < to_col(counts_ref[...])
    id_hi, id_lo = lax.shift_right_logical(ids, 7), lax.bitwise_and(ids, 127)
    book = jnp.concatenate([lax.shift_right_logical(home, 7), lax.bitwise_and(home, 127)], 1)
    book = book.astype(F32).astype(BF16)
    n_hi = home.shape[0]
    lane = iota((qd, META), 1)
    meta_hi = jnp.zeros((qd, META), F32)
    meta_lo = jnp.zeros((qd, META), F32)
    owner = None
    for k in range(slots):
        pick = one_hot(id_hi[:, k : k + 1] == iota((qd, n_hi), 1))
        found = nn(pick, book)
        found = found[:, :128] * 128.0 + found[:, 128:]
        found = jnp.where(id_lo[:, k : k + 1] == iota((qd, 128), 1), found, 0.0)
        row = jnp.sum(found, 1, keepdims=True).astype(I32)
        if owner is None:
            owner = lax.shift_right_logical(row, 10)
        place = lax.bitwise_and(row, 1023)
        hi = jnp.where(live[:, k : k + 1], lax.shift_right_logical(place, 5), -1).astype(F32)
        lo = lax.bitwise_and(place, 31).astype(F32)
        meta_hi = jnp.where(lane == k, hi, meta_hi)
        meta_lo = jnp.where(lane == k, lo, meta_lo)
    meta_hi, meta_lo = meta_hi.astype(BF16), meta_lo.astype(BF16)

    def message_rows(who, c):
        t, i = iota((n_msg, qd), 0), iota((n_msg, qd), 1)
        return one_hot(
            (lax.shift_right_logical(t, 4) == who)
            & (lax.bitwise_and(lax.shift_right_logical(t, 2), 3) == c)
            & (lax.bitwise_and(t, 3) == lax.bitwise_and(i, 3))
        )

    def query_rows(who, c):
        i, t = iota((qd, n_msg), 0), iota((qd, n_msg), 1)
        return one_hot(
            (lax.shift_right_logical(t, 4) == who)
            & (lax.bitwise_and(lax.shift_right_logical(t, 2), 3) == c)
            & (lax.bitwise_and(t, 3) == lax.bitwise_and(i, 3))
        )

    width = 256

    def fill(buf, mats, src):
        def body(t):
            at = pl.multiple_of(t * width, width)
            total = nn(mats[0], src[pl.ds(0, qd), pl.ds(at, width)])
            for c in range(1, PIECES):
                total += nn(mats[c], src[pl.ds(0, qd), pl.ds(pl.multiple_of(at + c * piece, width), width)])
            buf[:, pl.ds(at, width)] = total.astype(BF16)

        loop(piece // width, body)

    def deliver(out, inn, send, recv):
        def copy(j, frm):
            to = lax.rem(dp + j, n_dp)
            return remote(
                out.at[pl.ds(pl.multiple_of(to * 16, 16), 16)],
                inn.at[pl.ds(pl.multiple_of(frm * 16, 16), 16)],
                send.at[j], recv.at[j], (to, me),
            )

        def came(j):
            return copy(j, lax.rem(dp + n_dp - j, n_dp))

        def begin():
            loop(n_dp - 1, lambda j: copy(j + 1, dp).start())
            mine = pl.ds(pl.multiple_of(dp * 16, 16), 16)
            inn[mine, :] = out[mine, :]

        def arrived():
            loop(n_dp - 1, lambda j: came(j + 1).wait_recv())

        def sent():
            loop(n_dp - 1, lambda j: came(j + 1).wait_send())

        return begin, arrived, sent

    request, request_in, request_sent = deliver(req_out, req_in, rq_s, rq_r)
    answer, answer_in, answer_sent = deliver(ret_out, ret_in, rt_s, rt_r)

    q_in.wait()
    owner_row = to_row(owner)
    pack = [message_rows(owner_row, c) for c in range(PIECES)]
    fill(req_out, pack, qv)
    req_out[:, piece:] = (nn(pack[0], meta_hi) + nn(pack[1], meta_lo)).astype(BF16)
    request()

    def scores(at, n):
        def body(t):
            cols = pl.ds(pl.multiple_of(t * width, width), width)
            s_ref[pl.ds(at, n), cols] = SCALE * nt(qv[pl.ds(at, n), :], pv[cols, :])

        loop(pd // width, body)
        s = s_ref[pl.ds(at, n), :]
        top = jnp.max(s, 1, keepdims=True)
        e = jnp.exp(s - top)
        mcol[pl.ds(at, n), :] = jnp.broadcast_to(top, (n, 128))
        lcol[pl.ds(at, n), :] = jnp.broadcast_to(jnp.sum(e, 1, keepdims=True), (n, 128))
        e_ref[pl.ds(0, n), :] = e.astype(BF16)

    def sums(n, dst, at):
        def body(t):
            cols = pl.ds(pl.multiple_of(t * 512, 512), 512)
            dst[pl.ds(at, n), cols] = nn(e_ref[pl.ds(0, n), :], pv[:, cols]).astype(dst.dtype)

        loop(d // 512, body)

    def chunk(slot, part):
        scores(slot * qd + part * half, half)
        sums(half, ob, (slot - 1) * qd + part * half)

    p_in.wait()
    scores(0, qd)
    sums(qd, base, 0)

    ag_r1.wait_recv()
    ag_r3.start()
    ag_l1.wait_recv()
    ag_l3.start()
    chunk(1, 0)
    chunk(2, 1)

    request_in()
    t_in.wait()
    unpack = [query_rows(lax.shift_right_logical(iota((qd, 1), 0), 2), c) for c in range(PIECES)]

    def unpack_body(t):
        at = pl.multiple_of(t * width, width)
        for c in range(PIECES):
            cols = pl.ds(pl.multiple_of(at + c * piece, width), width)
            qr[:, cols] = nn(unpack[c], req_in[:, pl.ds(at, width)]).astype(BF16)

    loop(piece // width, unpack_body)
    tail = req_in[:, piece:]
    places = nn(unpack[0], tail) * 32.0 + nn(unpack[1], tail)
    mcol[pl.ds(nx * qd, qd), :] = places

    def neg_scores(t):
        cols = pl.ds(pl.multiple_of(t * width, width), width)
        sneg[:, cols] = SCALE * nt(qr[...], tv[cols, :])

    n_rows = tv.shape[0]
    loop(n_rows // width, neg_scores)

    def neg_weights(t):
        at = pl.ds(pl.multiple_of(t * 16, 16), 16)
        where = mcol[pl.ds(pl.multiple_of(nx * qd + t * 16, 16), 16), :]
        s = sneg[at, :]
        col = iota((16, n_rows), 1).astype(F32)
        times = jnp.zeros((16, n_rows), F32)
        for k in range(slots):
            times += jnp.where(where[:, k : k + 1] == col, 1.0, 0.0)
        named = times > 0.0
        top = jnp.max(jnp.where(named, s, -jnp.inf), 1, keepdims=True)
        e = jnp.where(named, times * jnp.exp(jnp.where(named, s - top, 0.0)), 0.0)
        eneg[at, :] = e.astype(BF16)
        sneg[at, pl.ds(0, 128)] = jnp.broadcast_to(top, (16, 128))
        sneg[at, pl.ds(128, 128)] = jnp.broadcast_to(jnp.sum(e, 1, keepdims=True), (16, 128))

    loop(qd // 16, neg_weights)

    def neg_sums(t):
        cols = pl.ds(pl.multiple_of(t * 512, 512), 512)
        oneg[:, cols] = nn(eneg[...], tv[:, cols]).astype(BF16)

    loop(d // 512, neg_sums)
    back = [message_rows(lax.shift_right_logical(iota((1, qd), 1), 2), c) for c in range(PIECES)]
    fill(ret_out, back, oneg)
    rest = jnp.where(lane == 0, sneg[:, :128], jnp.where(lane == 1, sneg[:, 128:256], 0.0))
    tail = jnp.zeros((n_msg, META), F32)
    for c in range(3):
        part = rest.astype(BF16)
        rest = rest - part.astype(F32)
        tail += nn(back[c], part)
    ret_out[:, piece:] = tail.astype(BF16)
    answer()

    ag_r2.wait_recv()
    chunk(1, 1)
    ag_l2.wait_recv()
    chunk(2, 0)

    def back_step(i, src, dst, peer):
        return remote(src, dst, rs_s.at[i], rs_r.at[i], peer)

    def ob_rows(slot, part, k=0, n=half):
        return pl.ds((slot - 1) * qd + part * half + k * sub, n)

    ag_r3.wait_recv()
    b_r = back_step(0, ob.at[ob_rows(2, 1)], grecv.at[0, pl.ds(half, half)], right)
    b_r.start()
    ag_l3.wait_recv()
    b_l = back_step(1, ob.at[ob_rows(1, 0)], grecv.at[1, pl.ds(0, half)], left)
    b_l.start()
    a_r, a_l, c_r, c_l = [], [], [], []
    for k in range(SUBS):
        a_r.append(back_step(2 + 4 * k, ob.at[ob_rows(3, 0, k, sub)], arecv.at[0, pl.ds(k * sub, sub)], right))
        a_l.append(back_step(3 + 4 * k, ob.at[ob_rows(3, 1, k, sub)], arecv.at[1, pl.ds(k * sub, sub)], left))
        c_r.append(back_step(4 + 4 * k, ob.at[ob_rows(2, 0, k, sub)], grecv.at[0, pl.ds(k * sub, sub)], right))
        c_l.append(
            back_step(5 + 4 * k, ob.at[ob_rows(1, 1, k, sub)], grecv.at[1, pl.ds(half + k * sub, sub)], left)
        )
    chunk(3, 0)
    for k in range(SUBS):
        a_r[k].start()
    chunk(3, 1)
    for k in range(SUBS):
        a_l[k].start()

    for entry, slot in enumerate((2, 3, 1, 3)):
        at = pl.ds(slot * qd, qd)
        m_row, l_row = to_row(mcol[at, :1]), to_row(lcol[at, :1])
        st_out[entry, :, :] = jnp.where(iota((8, qd), 0) == 0, m_row, l_row)
    st_right = remote(st_out.at[pl.ds(0, 2)], st_in.at[pl.ds(0, 2)], st_s.at[0], st_r.at[0], right)
    st_left = remote(st_out.at[pl.ds(2, 2)], st_in.at[pl.ds(2, 2)], st_s.at[1], st_r.at[1], left)
    st_across = remote(st_out.at[pl.ds(1, 1)], st_in.at[pl.ds(4, 1)], st_s.at[2], st_r.at[2], across)
    for copy in (st_right, st_left, st_across):
        copy.start()

    answer_in()
    opened = [query_rows(owner, c) for c in range(PIECES)]
    tail = ret_in[:, piece:]
    neg_stats = nn(opened[0], tail) + nn(opened[1], tail) + nn(opened[2], tail)
    for copy in (st_right, st_left, st_across):
        copy.wait_recv()

    def stat(entry, i):
        return to_col(st_in[entry, i : i + 1, :])

    m_own, l_own = mcol[pl.ds(0, qd), :1], lcol[pl.ds(0, qd), :1]
    m_l, l_l, m_r, l_r, m_x, l_x = (stat(e, i) for e in (0, 2, 4) for i in (0, 1))
    m_n, l_n = neg_stats[:, 0:1], neg_stats[:, 1:2]
    pairs = ((m_own, l_own), (m_l, l_l), (m_r, l_r), (m_x, l_x), (m_n, l_n))
    top = functools.reduce(jnp.maximum, [m for m, _ in pairs])
    lse = top + jnp.log(sum(l * jnp.exp(m - top) for m, l in pairs))
    lse_row = to_row(lse)
    lse_out[...] = jnp.broadcast_to(lse_row, (8, qd))
    lse_copies = [
        remote(lse_out, lse_in.at[i], ls_s.at[i], ls_r.at[i], peer)
        for i, peer in enumerate((right, left, across))
    ]
    for copy in lse_copies:
        copy.start()
    eye = iota((qd, qd), 0) == iota((qd, qd), 1)
    positive = jnp.sum(jnp.where(eye, s_ref[pl.ds(0, qd), pl.ds(0, qd)], 0.0), 0, keepdims=True)
    loss_ref[...] = lse_row - positive

    f_own, f_n = jnp.exp(m_own - lse), jnp.exp(m_n - lse)

    def base_body(t):
        at = pl.multiple_of(t * width, width)
        for c in range(PIECES):
            cols = pl.ds(pl.multiple_of(at + c * piece, width), width)
            neg = nn(opened[c], ret_in[:, pl.ds(at, width)])
            base[:, cols] = f_own * base[:, cols] + f_n * neg - pv[pl.ds(0, qd), cols].astype(F32)

    loop(piece // width, base_body)

    w_ref[pl.ds(0, qd), :] = jnp.exp(s_ref[pl.ds(0, qd), :] - lse).astype(BF16)
    for i in range(3):
        lse_copies[i].wait_recv()
        at = pl.ds((i + 1) * qd, qd)
        w_ref[at, :] = jnp.exp(s_ref[at, :] - to_col(lse_in[i, 0:1, :])).astype(BF16)
    spill = pltpu.make_async_copy(qv, qall_hbm, out_sem.at[0])
    spill.start()

    def merge(slot, part, m_far, src):
        m_near = mcol[pl.ds(slot * qd + part * half, half), :1]
        m_far = m_far[part * half : (part + 1) * half]
        both = jnp.maximum(m_near, m_far)
        f_near, f_far = jnp.exp(m_near - both), jnp.exp(m_far - both)

        def add(k):
            at = ob_rows(slot, part, k, sub)
            near, far = f_near[k * sub : (k + 1) * sub], f_far[k * sub : (k + 1) * sub]

            def body(t):
                cols = pl.ds(pl.multiple_of(t * 512, 512), 512)
                total = near * ob[at, cols].astype(F32) + far * src[pl.ds(k * sub, sub), cols].astype(F32)
                ob[at, cols] = total.astype(BF16)

            loop(d // 512, body)

        return add

    merge_r = merge(2, 0, stat(1, 0), arecv.at[0])
    merge_l = merge(1, 1, stat(3, 0), arecv.at[1])
    for k in range(SUBS):
        a_r[k].wait_recv()
        merge_r(k)
        c_r[k].start()
        a_l[k].wait_recv()
        merge_l(k)
        c_l[k].start()

    top_l, top_r = jnp.maximum(m_l, m_x), jnp.maximum(m_r, m_x)
    first = iota((qd, 1), 0) < half
    f_l = jnp.exp(jnp.where(first, top_l, m_l) - lse)
    f_r = jnp.exp(jnp.where(first, m_r, top_r) - lse)

    def finish(at, n):
        near_l, near_r = f_l[at : at + n], f_r[at : at + n]

        def body(t):
            cols = pl.ds(pl.multiple_of(t * 512, 512), 512)
            total = base[pl.ds(at, n), cols]
            total += near_l * grecv[0, pl.ds(at, n), cols].astype(F32)
            total += near_r * grecv[1, pl.ds(at, n), cols].astype(F32)
            gq_ref[pl.ds(at, n), cols] = (SCALE * total).astype(BF16)

        loop(d // 512, body)

    b_r.wait_recv()
    b_l.wait_recv()
    for k in range(SUBS):
        c_r[k].wait_recv()
        finish(k * sub, sub)
        c_l[k].wait_recv()
        finish(half + k * sub, sub)

    spill.wait()
    for copy in (ag_r1, ag_r2, ag_r3, ag_l1, ag_l2, ag_l3, b_r, b_l, *a_r, *a_l, *c_r, *c_l):
        copy.wait_send()
    for copy in (st_right, st_left, st_across, *lse_copies):
        copy.wait_send()
    request_sent()
    answer_sent()


def passage_kernel(w_ref, q_ref, gq_in, gp_ref, gq_ref):
    qd = gq_in.shape[0]
    total = tn(w_ref[...], q_ref[...])
    gp_ref[...] = (SCALE * total).astype(BF16)
    gp_ref[pl.ds(0, qd), :] = (SCALE * (total[:qd] - q_ref[pl.ds(0, qd), :].astype(F32))).astype(BF16)
    gq_ref[...] = gq_in[...]


def per_device(n_dp, queries, passages, neg_table, neg_ids, counts, neg_home):
    qd, d = queries.shape
    pd = passages.shape[0]
    n_rows = neg_table.shape[0]
    nx, half = 4, qd // 2
    n_msg, piece = n_dp * 16, d // PIECES
    any_spec = pl.BlockSpec(memory_space=pl.ANY)
    vmem_spec = pl.BlockSpec(memory_space=pltpu.VMEM)
    dma = pltpu.SemaphoreType.DMA
    qall, w, gq, loss = pl.pallas_call(
        functools.partial(exchange_kernel, n_dp),
        out_shape=(
            jax.ShapeDtypeStruct((nx * qd, d), BF16),
            jax.ShapeDtypeStruct((nx * qd, pd), BF16),
            jax.ShapeDtypeStruct((qd, d), BF16),
            jax.ShapeDtypeStruct((1, qd), F32),
        ),
        in_specs=[any_spec] * 3 + [vmem_spec] * 3,
        out_specs=(any_spec, vmem_spec, vmem_spec, vmem_spec),
        scratch_shapes=[
            pltpu.VMEM((nx * qd, d), BF16),
            pltpu.VMEM((pd, d), BF16),
            pltpu.VMEM((n_rows, d), BF16),
            pltpu.VMEM((nx * qd, pd), F32),
            pltpu.VMEM((qd, pd), BF16),
            pltpu.VMEM(((nx + 1) * qd, 128), F32),
            pltpu.VMEM((nx * qd, 128), F32),
            pltpu.VMEM(((nx - 1) * qd, d), BF16),
            pltpu.VMEM((qd, d), F32),
            pltpu.VMEM((2, half, d), BF16),
            pltpu.VMEM((2, qd, d), BF16),
            pltpu.VMEM((n_msg, piece + META), BF16),
            pltpu.VMEM((n_msg, piece + META), BF16),
            pltpu.VMEM((n_msg, piece + META), BF16),
            pltpu.VMEM((n_msg, piece + META), BF16),
            pltpu.VMEM((qd, d), BF16),
            pltpu.VMEM((qd, n_rows), F32),
            pltpu.VMEM((qd, n_rows), BF16),
            pltpu.VMEM((qd, d), BF16),
            pltpu.VMEM((4, 8, qd), F32),
            pltpu.VMEM((5, 8, qd), F32),
            pltpu.VMEM((8, qd), F32),
            pltpu.VMEM((3, 8, qd), F32),
            dma((3,)),
            dma((1,)),
            dma((6,)),
            dma((6,)),
            dma((2 + 4 * SUBS,)),
            dma((2 + 4 * SUBS,)),
            dma((3,)),
            dma((3,)),
            dma((3,)),
            dma((3,)),
            dma((n_dp,)),
            dma((n_dp,)),
            dma((n_dp,)),
            dma((n_dp,)),
        ],
        compiler_params=pltpu.CompilerParams(
            collective_id=0, has_side_effects=True, vmem_limit_bytes=56 * 1024 * 1024
        ),
        cost_estimate=pl.CostEstimate(flops=9_000_000_000, bytes_accessed=25_000_000, transcendentals=1_000_000),
        name="exchange",
    )(queries, passages, neg_table, neg_ids, counts.reshape(1, qd), neg_home.reshape(-1, 128))
    tile = 512
    grad_p, grad_q = pl.pallas_call(
        passage_kernel,
        grid=(d // tile,),
        out_shape=(jax.ShapeDtypeStruct((pd, d), BF16), jax.ShapeDtypeStruct((qd, d), BF16)),
        in_specs=[
            pl.BlockSpec((nx * qd, pd), lambda t: (0, 0)),
            pl.BlockSpec((nx * qd, tile), lambda t: (0, t)),
            pl.BlockSpec((qd, tile), lambda t: (0, t)),
        ],
        out_specs=(
            pl.BlockSpec((pd, tile), lambda t: (0, t)),
            pl.BlockSpec((qd, tile), lambda t: (0, t)),
        ),
        compiler_params=pltpu.CompilerParams(vmem_limit_bytes=32 * 1024 * 1024),
        cost_estimate=pl.CostEstimate(flops=3_300_000_000, bytes_accessed=14_000_000, transcendentals=0),
        name="passage_grads",
    )(w, qall, gq)
    return loss.reshape(qd), grad_q, grad_p


def solution(mesh):
    in_specs = (
        P(("dp", "blk"), None),
        P(("dp", "blk"), None),
        P("dp", None),
        P(("dp", "blk"), None),
        P(("dp", "blk")),
        P(),
    )
    out_specs = (P(("dp", "blk")), P(("dp", "blk"), None), P(("dp", "blk"), None))
    return jax.shard_map(
        functools.partial(per_device, mesh.shape["dp"]),
        mesh=mesh, in_specs=in_specs, out_specs=out_specs, check_vma=False,
    )
```

time: 530 us -> 116 us (0.22); the launches traced: 522 us -> 116 us
  waiting for transfers between devices: 325 us -> 0 us
  Pallas kernels: 0 us -> 109 us
  matrix products: 80.2 us -> 0 us
  local copies, waits for them, and re-layouts: 61.5 us -> 6.48 us
  blocking collectives: 22.8 us -> 0 us
  starting transfers between devices: 16.1 us -> 0 us
  other arithmetic: 15.2 us -> 0 us
    all_to_all x1 -> x0, waiting for transfers between devices: 187 us -> none  [fetch_negatives(): lax.all_to_all(found, 'dp', split_axis=0, concat_axis=0, tiled=True)]
    ppermute x11 -> x0, waiting for transfers between devices: 139 us -> none  [from_behind(): return lax.ppermute(block, axis, route)]
    pallas_call x0 -> x2, Pallas kernels: none -> 109 us  [the longest x1 102 us: per_device(): pl.pallas_call(functools.partial(exchange_kernel, n_dp), out_shape=(jax.S...]
    dot_general x14 -> x0, matrix products: 80.2 us -> none  [the longest x4 38.7 us: per_device(): lax.dot_general(weights, kept_blocks[step], (((0,), (0,)), ((), ())), pre...]
    gather x5 -> x0, local copies, waits for them, and re-layouts: 58.6 us -> none  [the longest x1 33.1 us: fetch_negatives(): neg_table[lax.all_to_all(request, 'dp', split_axis=0, concat_axis=0, tile...]
    all_to_all x1 -> x0, blocking collectives: 15.6 us -> none  [fetch_negatives(): lax.all_to_all(request, 'dp', split_axis=0, concat_axis=0, tiled=True)]
    ppermute x11 -> x0, starting transfers between devices: 10.8 us -> none  [from_behind(): return lax.ppermute(block, axis, route)]
    convert_element_type x2 -> x0, other arithmetic: 8.24 us -> none  [the longest x1 8.24 us: per_device(): return (loss, summed.astype(jnp.bfloat16), grad_p.astype(jnp.bfloat16))]
  transfers between devices with their start and end apart: 12 -> 0, of which waited for: 8 -> 0; matrix products, arithmetic and copies ran while one was open for 18% -> 0% of each run, Pallas kernels for 0% -> 0%
where the time goes in v1:
time: 116 us
  Pallas kernels  109 us (94%)
  local copies, waits for them, and re-layouts  6.48 us (6%)
    pallas_call x1, Pallas kernels, per_device(): pl.pallas_call(functools.partial(exchange_kernel, n_dp), out_shape=(jax.S...  102 us
    pallas_call x1, Pallas kernels, per_device(): pl.pallas_call(passage_kernel, grid=(d // tile,), out_shape=(jax.ShapeDty...  6.86 us
    unnamed x10, local copies, waits for them, and re-layouts  6.48 us

profile of v1, /device:TPU:0, one launch (start us, length us, event | category | flops | bytes accessed | tf_op | source)
XLA Modules:
  0.0 116.0 jit_solution(12731439172789862209)
XLA Ops:
  0.6 1.4 %copy.9.ids_ref = s32[128,16]{1,0:T(8,128)} copy(s32[128,16]{0,1:T(8,128)} %param.9) | data formatting | bytes 16384 | tf_op args[3]
  2.1 102.0 %exchange.1 = (bf16[512,4096]{1,0:T(8,128)(2,1)}, bf16[512,768]{1,0:T(8,128)(2,1)}, bf16[128,4096]{1,0:T(8,128)(2,1)}, f32[1,128]{1,0:T(1,128)}) custom-call(bf16[128,4096]{1,0:T(8,128)(2,1)} %q_hbm.1, bf16[768,4096]{1,0:T(8,128)(2,1)} %p_hbm.1, bf16[1024,4096]{1,0:T(8,128)(2,1)} %t_hbm.1, s32[128,16]{1,0:T(8,128)} %copy.9.ids_ref, s32[1,128]{1,0:T(1,128)} %bitcast.4, ...), custom_call_target="tpu_custom_call" | custom-call | flops 8999999488 | bytes 25000000 | tf_op jit(solution)/shard_map/exchange/pallas_call | solution.py:461
  104.1 0.0 copy-start.3
  104.1 0.0 copy-start
  104.1 2.2 %copy-done = bf16[512,4096]{1,0:T(8,128)(2,1)S(1)} copy-done((bf16[512,4096]{1,0:T(8,128)(2,1)S(1)}, bf16[512,4096]{1,0:T(8,128)(2,1)}, u32[]{:S(2)}) %copy-start) | copy-done | bytes 4194328
  106.3 0.0 copy-start.1
  106.3 1.2 %copy-done.1 = bf16[128,4096]{1,0:T(8,128)(2,1)S(1)} copy-done((bf16[128,4096]{1,0:T(8,128)(2,1)S(1)}, bf16[128,4096]{1,0:T(8,128)(2,1)}, u32[]{:S(2)}) %copy-start.1) | copy-done | bytes 1048600
  107.5 0.0 copy-start.2
  107.5 1.1 copy-done.2
  108.6 6.9 %passage_grads.1 = (bf16[768,4096]{1,0:T(8,128)(2,1)}, bf16[128,4096]{1,0:T(8,128)(2,1)}) custom-call(bf16[512,768]{1,0:T(8,128)(2,1)S(1)} %copy-done.2, bf16[512,4096]{1,0:T(8,128)(2,1)S(1)} %copy-done, bf16[128,4096]{1,0:T(8,128)(2,1)S(1)} %copy-done.1), custom_call_target="tpu_custom_call" | custom-call | flops 3300000000 | bytes 14000000 | tf_op jit(solution)/shard_map/passage_grads/pallas_call | solution.py:517
  115.5 0.0 copy-done.3
  115.5 0.5 copy.11
Async XLA Ops:
  104.1 11.4 %copy-start.3 = (f32[1,128]{1,0:T(1,128)S(1)}, f32[1,128]{1,0:T(1,128)}, u32[]{:S(2)}) copy-start(f32[1,128]{1,0:T(1,128)} %get-tuple-element.9) | copy-start | bytes 1540
  104.1 2.2 %copy-start = (bf16[512,4096]{1,0:T(8,128)(2,1)S(1)}, bf16[512,4096]{1,0:T(8,128)(2,1)}, u32[]{:S(2)}) copy-start(bf16[512,4096]{1,0:T(8,128)(2,1)} %get-tuple-element.11.q_ref) | copy-start | bytes 12582916
  106.3 1.2 %copy-start.1 = (bf16[128,4096]{1,0:T(8,128)(2,1)S(1)}, bf16[128,4096]{1,0:T(8,128)(2,1)}, u32[]{:S(2)}) copy-start(bf16[128,4096]{1,0:T(8,128)(2,1)} %get-tuple-element.12.gq_in) | copy-start | bytes 3145732
  107.5 1.1 copy-start.2

commit v2 on v1

v2 whole, which is shorter than its diff:
```python
import functools

import jax
import jax.numpy as jnp
from jax import lax
from jax.experimental import pallas as pl
from jax.experimental.pallas import tpu as pltpu
from jax.sharding import PartitionSpec as P

MESH = pl.DeviceIdType.MESH
F32, BF16, I32 = jnp.float32, jnp.bfloat16, jnp.int32
SCALE = 0.0625
META = 128
PIECES = 4
SUBS = 4


def nn(a, b):
    return jnp.dot(a, b, preferred_element_type=F32)


def nt(a, b):
    return lax.dot_general(a, b, (((1,), (1,)), ((), ())), preferred_element_type=F32)


def tn(a, b):
    return lax.dot_general(a, b, (((0,), (0,)), ((), ())), preferred_element_type=F32)


def iota(shape, dim):
    return lax.broadcasted_iota(I32, shape, dim)


def to_row(col):
    n = col.shape[0]
    eye = iota((n, n), 0) == iota((n, n), 1)
    return jnp.sum(jnp.where(eye, col, jnp.zeros_like(col)), 0, keepdims=True)


def to_col(row):
    n = row.shape[1]
    eye = iota((n, n), 0) == iota((n, n), 1)
    return jnp.sum(jnp.where(eye, row, jnp.zeros_like(row)), 1, keepdims=True)


def one_hot(cond):
    return jnp.where(cond, 1.0, 0.0).astype(BF16)


def loop(n, body):
    lax.fori_loop(0, n, lambda t, carry: (body(t), carry)[1], 0)


def message_rows(n_msg, who, c):
    t, i = iota((n_msg, who.shape[1]), 0), iota((n_msg, who.shape[1]), 1)
    return one_hot(
        (lax.shift_right_logical(t, 4) == who)
        & (lax.bitwise_and(lax.shift_right_logical(t, 2), 3) == c)
        & (lax.bitwise_and(t, 3) == lax.bitwise_and(i, 3))
    )


def query_rows(n_msg, who, c):
    i, t = iota((who.shape[0], n_msg), 0), iota((who.shape[0], n_msg), 1)
    return one_hot(
        (lax.shift_right_logical(t, 4) == who)
        & (lax.bitwise_and(lax.shift_right_logical(t, 2), 3) == c)
        & (lax.bitwise_and(t, 3) == lax.bitwise_and(i, 3))
    )


def exchange_kernel(
    n_dp, q_hbm, p_hbm, t_hbm, ids_ref, counts_ref, home_ref,
    gp_ref, gq_ref, loss_ref,
    qv, pv, tv, s_ref, e_ref, wt_ref, stats, ob, base, arecv, grecv,
    req_out, req_in, ret_out, ret_in, qr, sneg, times_ref, eneg, oneg, factors,
    st_out, st_in, lse_out, lse_in,
    local_sem, ag_s, ag_r, rs_s, rs_r, st_s, st_r, ls_s, ls_r,
    rq_s, rq_r, rt_s, rt_r,
):
    qd, d = q_hbm.shape
    pd = p_hbm.shape[0]
    half, piece = qd // 2, d // PIECES
    sub = half // SUBS
    slots = ids_ref.shape[0]
    n_msg = n_dp * 16
    nx = 4
    dp, me = lax.axis_index("dp"), lax.axis_index("blk")
    right = (dp, lax.rem(me + 1, nx))
    left = (dp, lax.rem(me + nx - 1, nx))
    across = (dp, lax.rem(me + 2, nx))

    barrier = pltpu.get_barrier_semaphore()
    for peer in (right, left, across):
        pl.semaphore_signal(barrier, inc=1, device_id=peer, device_id_type=MESH)

    def greet(j):
        peer = lax.rem(dp + j + 1, n_dp)
        pl.semaphore_signal(barrier, inc=1, device_id=(peer, me), device_id_type=MESH)

    loop(n_dp - 1, greet)
    q_in = pltpu.make_async_copy(q_hbm, qv.at[pl.ds(0, qd)], local_sem.at[0])
    p_in = pltpu.make_async_copy(p_hbm, pv, local_sem.at[1])
    t_in = pltpu.make_async_copy(t_hbm, tv, local_sem.at[2])
    q_in.start()
    p_in.start()
    t_in.start()
    pl.semaphore_wait(barrier, n_dp + 2)

    def remote(src, dst, send, recv, peer):
        return pltpu.make_async_remote_copy(
            src_ref=src, dst_ref=dst, send_sem=send, recv_sem=recv, device_id=peer, device_id_type=MESH
        )

    def half_rows(block, part, k=0, n=half):
        return pl.ds(block * qd + part * half + k * sub, n)

    def gather_step(i, src, block, part, peer):
        return remote(src, qv.at[half_rows(block, part)], ag_s.at[i], ag_r.at[i], peer)

    own = [q_hbm.at[pl.ds(0, half)], q_hbm.at[pl.ds(half, half)]]
    ag_r1 = gather_step(0, own[0], 1, 0, right)
    ag_l1 = gather_step(1, own[1], 1, 1, left)
    ag_r2 = gather_step(2, own[1], 2, 1, right)
    ag_l2 = gather_step(3, own[0], 2, 0, left)
    ag_r3 = gather_step(4, qv.at[half_rows(1, 0)], 3, 0, right)
    ag_l3 = gather_step(5, qv.at[half_rows(1, 1)], 3, 1, left)
    for copy in (ag_r1, ag_l1, ag_r2, ag_l2):
        copy.start()

    ids, home = ids_ref[...], home_ref[...]
    book = jnp.concatenate([lax.shift_right_logical(home, 7), lax.bitwise_and(home, 127)], 1)
    book = book.astype(F32).T.astype(BF16)
    n_hi = home.shape[0]
    together = 4
    named_rows = []
    for k in range(0, slots, together):
        id_row = jnp.concatenate([ids[k + i : k + i + 1] for i in range(together)], 1)
        pick = one_hot(lax.shift_right_logical(id_row, 7) == iota((n_hi, together * qd), 0))
        found = nn(book, pick)
        found = found[:128] * 128.0 + found[128:]
        mine = lax.bitwise_and(id_row, 127) == iota((128, together * qd), 0)
        row = jnp.sum(jnp.where(mine, found, 0.0), 0, keepdims=True).astype(I32)
        named_rows += [row[:, i * qd : (i + 1) * qd] for i in range(together)]
    rows = jnp.zeros((slots, qd), I32)
    for k in range(slots):
        rows = jnp.where(iota((slots, qd), 0) == k, named_rows[k], rows)
    live = iota((slots, qd), 0) < counts_ref[...]
    place = lax.bitwise_and(rows, 1023)
    meta_hi = jnp.where(live, lax.shift_right_logical(place, 5), -1).astype(F32)
    meta_lo = lax.bitwise_and(place, 31).astype(F32)
    blank = jnp.zeros((META - slots, qd), F32)
    meta_hi = jnp.concatenate([meta_hi, blank], 0).astype(BF16)
    meta_lo = jnp.concatenate([meta_lo, blank], 0).astype(BF16)
    owner_row = lax.shift_right_logical(named_rows[0], 10)
    width = 512

    def fill(buf, mats, src):
        def body(t):
            at = pl.multiple_of(t * width, width)
            total = nn(mats[0], src[pl.ds(0, qd), pl.ds(at, width)])
            for c in range(1, PIECES):
                total += nn(mats[c], src[pl.ds(0, qd), pl.ds(pl.multiple_of(at + c * piece, width), width)])
            buf[:, pl.ds(at, width)] = total.astype(BF16)

        loop(piece // width, body)

    def deliver(out, inn, send, recv):
        def copy(j, frm):
            to = lax.rem(dp + j, n_dp)
            return remote(
                out.at[pl.ds(pl.multiple_of(to * 16, 16), 16)],
                inn.at[pl.ds(pl.multiple_of(frm * 16, 16), 16)],
                send.at[j], recv.at[j], (to, me),
            )

        def came(j):
            return copy(j, lax.rem(dp + n_dp - j, n_dp))

        def begin():
            loop(n_dp - 1, lambda j: copy(j + 1, dp).start())
            mine = pl.ds(pl.multiple_of(dp * 16, 16), 16)
            inn[mine, :] = out[mine, :]

        def arrived():
            loop(n_dp - 1, lambda j: came(j + 1).wait_recv())

        def sent():
            loop(n_dp - 1, lambda j: came(j + 1).wait_send())

        return begin, arrived, sent

    request, request_in, request_sent = deliver(req_out, req_in, rq_s, rq_r)
    answer, answer_in, answer_sent = deliver(ret_out, ret_in, rt_s, rt_r)

    q_in.wait()
    pack = [message_rows(n_msg, owner_row, c) for c in range(PIECES)]
    fill(req_out, pack, qv)
    req_out[:, piece:] = (nt(pack[0], meta_hi) + nt(pack[1], meta_lo)).astype(BF16)
    request()

    def scores(block):
        cols = pl.ds(block * qd, qd)
        s_ref[:, cols] = SCALE * nt(pv[...], qv[cols, :])
        s = s_ref[:, cols]
        top = jnp.max(s, 0, keepdims=True)
        e = jnp.exp(s - top)
        stats[block, 0:1, :] = top
        stats[block, 1:2, :] = jnp.sum(e, 0, keepdims=True)
        for j in range(pd // 128):
            e_ref[:, j * 128 : (j + 1) * 128] = e[j * 128 : (j + 1) * 128].T.astype(BF16)

    wide = 2048

    def sums(dst, at):
        def body(t):
            cols = pl.ds(pl.multiple_of(t * wide, wide), wide)
            dst[pl.ds(at, qd), cols] = nn(e_ref[...], pv[:, cols]).astype(dst.dtype)

        loop(d // wide, body)

    p_in.wait()
    scores(0)
    sums(base, 0)

    ag_r1.wait_recv()
    ag_r3.start()
    ag_l1.wait_recv()
    ag_l3.start()
    scores(1)
    sums(ob, 0)

    request_in()
    t_in.wait()
    asker = lax.shift_right_logical(iota((qd, 1), 0), 2)
    for c in range(PIECES):
        qr[:, c * piece : (c + 1) * piece] = nn(query_rows(n_msg, asker, c), req_in[:, :piece]).astype(BF16)
    asker = lax.shift_right_logical(iota((1, qd), 1), 2)
    back = [message_rows(n_msg, asker, c) for c in range(PIECES)]
    tail = req_in[:, piece:]
    places = tn(tail, back[0]) * 32.0 + tn(tail, back[1])
    sneg[...] = SCALE * nt(tv[...], qr[...])
    n_rows = tv.shape[0]

    def neg_top(t, top):
        at = pl.ds(pl.multiple_of(t * 128, 128), 128)
        index = (iota((128, qd), 0) + t * 128).astype(F32)
        times = jnp.zeros((128, qd), F32)
        for k in range(slots):
            times += jnp.where(places[k : k + 1] == index, 1.0, 0.0)
        times_ref[at, :] = times
        return jnp.maximum(top, jnp.max(jnp.where(times > 0.0, sneg[at, :], -jnp.inf), 0, keepdims=True))

    m_far = lax.fori_loop(0, n_rows // 128, neg_top, jnp.full((1, qd), -jnp.inf, F32))

    def neg_weights(t, total):
        at = pl.ds(pl.multiple_of(t * 128, 128), 128)
        times = times_ref[at, :]
        e = jnp.where(times > 0.0, times * jnp.exp(jnp.minimum(sneg[at, :] - m_far, 0.0)), 0.0)
        eneg[:, at] = e.T.astype(BF16)
        return total + jnp.sum(e, 0, keepdims=True)

    l_far = lax.fori_loop(0, n_rows // 128, neg_weights, jnp.zeros((1, qd), F32))

    def neg_sums(t):
        cols = pl.ds(pl.multiple_of(t * wide, wide), wide)
        oneg[:, cols] = nn(eneg[...], tv[:, cols]).astype(BF16)

    loop(d // wide, neg_sums)
    fill(ret_out, back, oneg)
    line = iota((META, qd), 0)
    rest = jnp.where(line == 0, m_far, jnp.where(line == 1, l_far, 0.0))
    tail = jnp.zeros((n_msg, META), F32)
    for c in range(3):
        part = rest.astype(BF16)
        rest = rest - part.astype(F32)
        tail += nt(back[c], part)
    ret_out[:, piece:] = tail.astype(BF16)
    answer()

    ag_r2.wait_recv()
    ag_l2.wait_recv()
    scores(2)
    sums(ob, qd)

    def back_step(i, block, part, k, n, dst, at, peer):
        src = ob.at[half_rows(block - 1, part, k, n)]
        return remote(src, dst.at[pl.ds(at, n)], rs_s.at[i], rs_r.at[i], peer)

    both, quarter = 2, half // 2
    b_r = [back_step(k, 1, 1, k * SUBS // 2, quarter, grecv.at[0], half + k * quarter, right) for k in range(both)]
    b_l = [back_step(2 + k, 1, 0, k * SUBS // 2, quarter, grecv.at[1], k * quarter, left) for k in range(both)]
    a_r = [back_step(4 + 4 * k, 3, 0, k, sub, arecv.at[0], k * sub, right) for k in range(SUBS)]
    a_l = [back_step(5 + 4 * k, 3, 1, k, sub, arecv.at[1], k * sub, left) for k in range(SUBS)]
    c_r = [back_step(6 + 4 * k, 2, 0, k, sub, grecv.at[0], k * sub, right) for k in range(SUBS)]
    c_l = [back_step(7 + 4 * k, 2, 1, k, sub, grecv.at[1], half + k * sub, left) for k in range(SUBS)]
    b_r[0].start()
    b_l[0].start()
    ag_r3.wait_recv()
    ag_l3.wait_recv()
    scores(3)

    first = iota((8, qd), 1) < half
    picks = [stats[block, :, :] for block in range(nx)]
    st_out[0, :, :] = jnp.where(first, picks[2], picks[1])
    st_out[1, :, :] = picks[3]
    st_out[2, :, :] = jnp.where(first, picks[1], picks[2])
    st_out[3, :, :] = picks[3]
    st_right = remote(st_out.at[pl.ds(0, 2)], st_in.at[pl.ds(0, 2)], st_s.at[0], st_r.at[0], right)
    st_left = remote(st_out.at[pl.ds(2, 2)], st_in.at[pl.ds(2, 2)], st_s.at[1], st_r.at[1], left)
    st_across = remote(st_out.at[pl.ds(1, 1)], st_in.at[pl.ds(4, 1)], st_s.at[2], st_r.at[2], across)
    st_copies = [st_right, st_left, st_across]
    for copy in st_copies:
        copy.start()
    sums(ob, 2 * qd)
    for k in range(SUBS):
        a_r[k].start()
        a_l[k].start()

    answer_in()
    tail = ret_in[:, piece:]
    neg_stats = tn(tail, pack[0]) + tn(tail, pack[1]) + tn(tail, pack[2])
    for copy in st_copies:
        copy.wait_recv()

    def stat(entry, i):
        return st_in[entry, i : i + 1, :]

    m_own, l_own = stats[0, 0:1, :], stats[0, 1:2, :]
    m_l, l_l, m_r, l_r, m_x, l_x = (stat(e, i) for e in (0, 2, 4) for i in (0, 1))
    m_n, l_n = neg_stats[0:1], neg_stats[1:2]
    pairs = ((m_own, l_own), (m_l, l_l), (m_r, l_r), (m_x, l_x), (m_n, l_n))
    top = functools.reduce(jnp.maximum, [m for m, _ in pairs])
    lse = top + jnp.log(sum(l * jnp.exp(m - top) for m, l in pairs))
    lse_out[...] = jnp.broadcast_to(lse, (8, qd))
    lse_copies = [
        remote(lse_out, lse_in.at[i], ls_s.at[i], ls_r.at[i], peer)
        for i, peer in enumerate((right, left, across))
    ]
    for copy in lse_copies:
        copy.start()
    eye = iota((qd, qd), 0) == iota((qd, qd), 1)
    loss_ref[...] = lse - jnp.sum(jnp.where(eye, s_ref[pl.ds(0, qd), pl.ds(0, qd)], 0.0), 0, keepdims=True)

    f_own, f_n = to_col(jnp.exp(m_own - lse)), to_col(jnp.exp(m_n - lse))
    owner_col = to_col(owner_row)
    for c in range(PIECES):
        cols = pl.ds(c * piece, piece)
        neg = nn(query_rows(n_msg, owner_col, c), ret_in[:, :piece])
        base[:, cols] = f_own * base[:, cols] + f_n * neg - pv[pl.ds(0, qd), cols].astype(F32)

    for copy in lse_copies:
        copy.wait_recv()
    front = iota((1, qd), 1) < half
    lse_l, lse_r, lse_x = (lse_in[i, 0:1, :] for i in range(3))
    by_block = (lse, jnp.where(front, lse_l, lse_r), jnp.where(front, lse_r, lse_l), lse_x)
    for block in range(nx):
        cols = pl.ds(block * qd, qd)
        wt_ref[:, cols] = jnp.exp(s_ref[:, cols] - by_block[block]).astype(BF16)
    span = 1024

    def passage_grads(t):
        cols = pl.ds(pl.multiple_of(t * span, span), span)
        total = nn(wt_ref[...], qv[:, cols])
        gp_ref[pl.ds(qd, pd - qd), cols] = (SCALE * total[qd:]).astype(BF16)
        gp_ref[pl.ds(0, qd), cols] = (SCALE * (total[:qd] - qv[pl.ds(0, qd), cols].astype(F32))).astype(BF16)

    loop(d // span, passage_grads)

    m_near = stats[2, 0:1, :]
    m_away = jnp.where(front, stat(1, 0), stat(3, 0))
    m_both = jnp.maximum(m_near, m_away)
    factors[0, :, :] = jnp.broadcast_to(to_col(jnp.exp(m_near - m_both)), (qd, 128))
    factors[1, :, :] = jnp.broadcast_to(to_col(jnp.exp(m_away - m_both)), (qd, 128))

    def merge(part, k):
        at, far_at = part * half + k * sub, pl.ds(k * sub, sub)
        f_near, f_away = factors[0, pl.ds(at, sub), :1], factors[1, pl.ds(at, sub), :1]

        def body(t):
            cols = pl.ds(pl.multiple_of(t * 1024, 1024), 1024)
            here = ob[pl.ds(qd + at, sub), cols].astype(F32)
            total = f_near * here + f_away * arecv[part, far_at, cols].astype(F32)
            ob[pl.ds(qd + at, sub), cols] = total.astype(BF16)

        loop(d // 1024, body)

    for k in range(SUBS):
        a_r[k].wait_send()
        a_l[k].wait_send()
    b_r[1].start()
    b_l[1].start()
    for k in range(SUBS):
        a_r[k].wait_recv()
        merge(0, k)
        c_r[k].start()
        a_l[k].wait_recv()
        merge(1, k)
        c_l[k].start()

    top_l, top_r = jnp.maximum(m_l, m_x), jnp.maximum(m_r, m_x)
    factors[2, :, :] = jnp.broadcast_to(to_col(jnp.exp(jnp.where(front, top_l, m_l) - lse)), (qd, 128))
    factors[3, :, :] = jnp.broadcast_to(to_col(jnp.exp(jnp.where(front, m_r, top_r) - lse)), (qd, 128))

    def finish(at):
        f_l, f_r = factors[2, pl.ds(at, sub), :1], factors[3, pl.ds(at, sub), :1]

        def body(t):
            cols = pl.ds(pl.multiple_of(t * 1024, 1024), 1024)
            total = base[pl.ds(at, sub), cols]
            total += f_l * grecv[0, pl.ds(at, sub), cols].astype(F32)
            total += f_r * grecv[1, pl.ds(at, sub), cols].astype(F32)
            gq_ref[pl.ds(at, sub), cols] = (SCALE * total).astype(BF16)

        loop(d // 1024, body)

    for copy in b_r + b_l:
        copy.wait_recv()
    for k in range(SUBS):
        c_r[k].wait_recv()
        finish(k * sub)
        c_l[k].wait_recv()
        finish(half + k * sub)

    for copy in [ag_r1, ag_r2, ag_r3, ag_l1, ag_l2, ag_l3] + b_r + b_l + c_r + c_l + st_copies + lse_copies:
        copy.wait_send()
    request_sent()
    answer_sent()


def write_kernel(gp_in, gq_in, loss_in, gp_out, gq_out, loss_out, sems):
    parts = 4
    n = gp_in.shape[0] // parts
    copies = [
        pltpu.make_async_copy(gp_in.at[pl.ds(i * n, n)], gp_out.at[pl.ds(i * n, n)], sems.at[i]) for i in range(parts)
    ]
    copies.append(pltpu.make_async_copy(gq_in, gq_out, sems.at[parts]))
    copies.append(pltpu.make_async_copy(loss_in, loss_out, sems.at[parts + 1]))
    for copy in copies:
        copy.start()
    for copy in copies:
        copy.wait()


def per_device(n_dp, queries, passages, neg_table, neg_ids, counts, neg_home):
    qd, d = queries.shape
    pd = passages.shape[0]
    n_rows = neg_table.shape[0]
    nx, half = 4, qd // 2
    n_msg, piece = n_dp * 16, d // PIECES
    any_spec = pl.BlockSpec(memory_space=pl.ANY)
    vmem_spec = pl.BlockSpec(memory_space=pltpu.VMEM)
    dma = pltpu.SemaphoreType.DMA
    grad_p, grad_q, loss = pl.pallas_call(
        functools.partial(exchange_kernel, n_dp),
        out_shape=(
            pltpu.VMEM((pd, d), BF16),
            pltpu.VMEM((qd, d), BF16),
            pltpu.VMEM((1, qd), F32),
        ),
        in_specs=[any_spec] * 3 + [vmem_spec] * 3,
        out_specs=(vmem_spec, vmem_spec, vmem_spec),
        scratch_shapes=[
            pltpu.VMEM((nx * qd, d), BF16),
            pltpu.VMEM((pd, d), BF16),
            pltpu.VMEM((n_rows, d), BF16),
            pltpu.VMEM((pd, nx * qd), F32),
            pltpu.VMEM((qd, pd), BF16),
            pltpu.VMEM((pd, nx * qd), BF16),
            pltpu.VMEM((nx, 8, qd), F32),
            pltpu.VMEM(((nx - 1) * qd, d), BF16),
            pltpu.VMEM((qd, d), F32),
            pltpu.VMEM((2, half, d), BF16),
            pltpu.VMEM((2, qd, d), BF16),
            pltpu.VMEM((n_msg, piece + META), BF16),
            pltpu.VMEM((n_msg, piece + META), BF16),
            pltpu.VMEM((n_msg, piece + META), BF16),
            pltpu.VMEM((n_msg, piece + META), BF16),
            pltpu.VMEM((qd, d), BF16),
            pltpu.VMEM((n_rows, qd), F32),
            pltpu.VMEM((n_rows, qd), F32),
            pltpu.VMEM((qd, n_rows), BF16),
            pltpu.VMEM((qd, d), BF16),
            pltpu.VMEM((4, qd, 128), F32),
            pltpu.VMEM((4, 8, qd), F32),
            pltpu.VMEM((5, 8, qd), F32),
            pltpu.VMEM((8, qd), F32),
            pltpu.VMEM((3, 8, qd), F32),
            dma((3,)),
            dma((6,)),
            dma((6,)),
            dma((4 + 4 * SUBS,)),
            dma((4 + 4 * SUBS,)),
            dma((3,)),
            dma((3,)),
            dma((3,)),
            dma((3,)),
            dma((n_dp,)),
            dma((n_dp,)),
            dma((n_dp,)),
            dma((n_dp,)),
        ],
        compiler_params=pltpu.CompilerParams(
            collective_id=0, has_side_effects=True, vmem_limit_bytes=54 * 1024 * 1024
        ),
        cost_estimate=pl.CostEstimate(flops=13_000_000_000, bytes_accessed=25_000_000, transcendentals=1_000_000),
        name="exchange",
    )(queries, passages, neg_table, neg_ids.T, counts.reshape(1, qd), neg_home.reshape(-1, 128))
    grad_p, grad_q, loss = pl.pallas_call(
        write_kernel,
        out_shape=(
            jax.ShapeDtypeStruct((pd, d), BF16),
            jax.ShapeDtypeStruct((qd, d), BF16),
            jax.ShapeDtypeStruct((1, qd), F32),
        ),
        in_specs=[any_spec] * 3,
        out_specs=(any_spec, any_spec, any_spec),
        scratch_shapes=[dma((6,))],
        compiler_params=pltpu.CompilerParams(vmem_limit_bytes=1024 * 1024),
        cost_estimate=pl.CostEstimate(flops=0, bytes_accessed=7_300_000, transcendentals=0),
        name="write",
    )(grad_p, grad_q, loss)
    return loss.reshape(qd), grad_q, grad_p


def solution(mesh):
    in_specs = (
        P(("dp", "blk"), None),
        P(("dp", "blk"), None),
        P("dp", None),
        P(("dp", "blk"), None),
        P(("dp", "blk")),
        P(),
    )
    out_specs = (P(("dp", "blk")), P(("dp", "blk"), None), P(("dp", "blk"), None))
    return jax.shard_map(
        functools.partial(per_device, mesh.shape["dp"]),
        mesh=mesh, in_specs=in_specs, out_specs=out_specs, check_vma=False,
    )
```

time: 116 us -> 91.8 us (0.79)
  Pallas kernels: 109 us -> 90.8 us
  local copies, waits for them, and re-layouts: 6.48 us -> 0 us
    pallas_call x2, Pallas kernels: 109 us -> 90.8 us  [the longest x1 87.8 us: per_device(): pl.pallas_call(functools.partial(exchange_kernel, n_dp), out_shape=(pltpu...]
    unnamed x10 -> x0, local copies, waits for them, and re-layouts: 6.48 us -> none
where the time goes in v2:
time: 91.8 us; the launch traced here: 91.6 us
  Pallas kernels  90.8 us (99%)
    pallas_call x1, Pallas kernels, per_device(): pl.pallas_call(functools.partial(exchange_kernel, n_dp), out_shape=(pltpu...  87.8 us
    pallas_call x1, Pallas kernels, per_device(): pl.pallas_call(write_kernel, out_shape=(jax.ShapeDtypeStruct((pd, d), BF1...  3.05 us

profile of v2, /device:TPU:0, one launch (start us, length us, event | category | flops | bytes accessed | tf_op | source)
XLA Modules:
  0.0 91.6 jit_solution(6383166441332175120)
XLA Ops:
  0.6 87.8 %exchange.1 = (bf16[768,4096]{1,0:T(8,128)(2,1)S(1)}, bf16[128,4096]{1,0:T(8,128)(2,1)S(1)}, f32[1,128]{1,0:T(1,128)S(1)}) custom-call(bf16[128,4096]{1,0:T(8,128)(2,1)} %q_hbm.1, bf16[768,4096]{1,0:T(8,128)(2,1)} %p_hbm.1, bf16[1024,4096]{1,0:T(8,128)(2,1)} %t_hbm.1, s32[16,128]{1,0:T(8,128)} %bitcast.5, s32[1,128]{1,0:T(1,128)} %bitcast.6, s32[256,128]{1,0:T(8,128)} %bitcast.4), custom_call_target="tpu_custom_call" | custom-call | flops 12999999488 | bytes 25000000 | tf_op jit(solution)/shard_map/exchange/pallas_call | solution.py:454
  88.4 3.1 %write.1 = (bf16[768,4096]{1,0:T(8,128)(2,1)}, bf16[128,4096]{1,0:T(8,128)(2,1)}, f32[1,128]{1,0:T(1,128)}) custom-call(bf16[768,4096]{1,0:T(8,128)(2,1)S(1)} %get-tuple-element.9.gp_in, bf16[128,4096]{1,0:T(8,128)(2,1)S(1)} %get-tuple-element.10.gq_in, f32[1,128]{1,0:T(1,128)S(1)} %get-tuple-element.11.loss_in), custom_call_target="tpu_custom_call" | custom-call | bytes 7300000 | tf_op jit(solution)/shard_map/write/pallas_call | solution.py:509

commit v3 on v2

--- a/solution.py
+++ b/solution.py
@@ -70,13 +70,13 @@
 
 
 def exchange_kernel(
-    n_dp, q_hbm, p_hbm, t_hbm, ids_ref, counts_ref, home_ref,
+    n_dp, q_hbm, p_hbm, t_hbm, ids_hbm, counts_hbm, home_hbm,
     gp_ref, gq_ref, loss_ref,
-    qv, pv, tv, s_ref, e_ref, wt_ref, stats, ob, base, arecv, grecv,
+    ids_ref, counts_ref, home_ref, qv, pv, tv, s_ref, e_ref, wt_ref, stats, ob, base, arecv, grecv,
     req_out, req_in, ret_out, ret_in, qr, sneg, times_ref, eneg, oneg, factors,
     st_out, st_in, lse_out, lse_in,
     local_sem, ag_s, ag_r, rs_s, rs_r, st_s, st_r, ls_s, ls_r,
-    rq_s, rq_r, rt_s, rt_r,
+    rq_s, rq_r, rt_s, rt_r, group_there, peers_there,
 ):
     qd, d = q_hbm.shape
     pd = p_hbm.shape[0]
@@ -91,21 +91,41 @@
     across = (dp, lax.rem(me + 2, nx))
 
     barrier = pltpu.get_barrier_semaphore()
-    for peer in (right, left, across):
-        pl.semaphore_signal(barrier, inc=1, device_id=peer, device_id_type=MESH)
+    first_plane = me == 0
+    plane = jnp.maximum(me, 1)
+
+    @pl.when(me != 0)
+    def _():
+        pl.semaphore_signal(barrier, inc=1, device_id=(dp, 0), device_id_type=MESH)
 
     def greet(j):
         peer = lax.rem(dp + j + 1, n_dp)
-        pl.semaphore_signal(barrier, inc=1, device_id=(peer, me), device_id_type=MESH)
+        pl.semaphore_signal(barrier, inc=1, device_id=(peer, plane), device_id_type=MESH)
 
     loop(n_dp - 1, greet)
+    small_in = [
+        pltpu.make_async_copy(src, dst, local_sem.at[3 + i])
+        for i, (src, dst) in enumerate(((ids_hbm, ids_ref), (counts_hbm, counts_ref), (home_hbm, home_ref)))
+    ]
+    for copy in small_in:
+        copy.start()
     q_in = pltpu.make_async_copy(q_hbm, qv.at[pl.ds(0, qd)], local_sem.at[0])
     p_in = pltpu.make_async_copy(p_hbm, pv, local_sem.at[1])
     t_in = pltpu.make_async_copy(t_hbm, tv, local_sem.at[2])
     q_in.start()
     p_in.start()
     t_in.start()
-    pl.semaphore_wait(barrier, n_dp + 2)
+
+    @pl.when(first_plane)
+    def _():
+        pl.semaphore_wait(barrier, nx - 1)
+        for b in range(1, nx):
+            pl.semaphore_signal(group_there, inc=1, device_id=(dp, b), device_id_type=MESH)
+
+    @pl.when(me != 0)
+    def _():
+        pl.semaphore_wait(group_there, 1)
+
 
     def remote(src, dst, send, recv, peer):
         return pltpu.make_async_remote_copy(
@@ -128,6 +148,8 @@
     for copy in (ag_r1, ag_l1, ag_r2, ag_l2):
         copy.start()
 
+    for copy in small_in:
+        copy.wait()
     ids, home = ids_ref[...], home_ref[...]
     book = jnp.concatenate([lax.shift_right_logical(home, 7), lax.bitwise_and(home, 127)], 1)
     book = book.astype(F32).T.astype(BF16)
@@ -197,6 +219,20 @@
     pack = [message_rows(n_msg, owner_row, c) for c in range(PIECES)]
     fill(req_out, pack, qv)
     req_out[:, piece:] = (nt(pack[0], meta_hi) + nt(pack[1], meta_lo)).astype(BF16)
+
+    @pl.when(me == 1)
+    def _():
+        pl.semaphore_wait(barrier, 2 * (n_dp - 1))
+        pl.semaphore_signal(peers_there, inc=1, device_id=(dp, 0), device_id_type=MESH)
+
+    @pl.when(me > 1)
+    def _():
+        pl.semaphore_wait(barrier, n_dp - 1)
+
+    @pl.when(first_plane)
+    def _():
+        pl.semaphore_wait(peers_there, 1)
+
     request()
 
     def scores(block):
@@ -357,16 +393,6 @@
     for block in range(nx):
         cols = pl.ds(block * qd, qd)
         wt_ref[:, cols] = jnp.exp(s_ref[:, cols] - by_block[block]).astype(BF16)
-    span = 1024
-
-    def passage_grads(t):
-        cols = pl.ds(pl.multiple_of(t * span, span), span)
-        total = nn(wt_ref[...], qv[:, cols])
-        gp_ref[pl.ds(qd, pd - qd), cols] = (SCALE * total[qd:]).astype(BF16)
-        gp_ref[pl.ds(0, qd), cols] = (SCALE * (total[:qd] - qv[pl.ds(0, qd), cols].astype(F32))).astype(BF16)
-
-    loop(d // span, passage_grads)
-
     m_near = stats[2, 0:1, :]
     m_away = jnp.where(front, stat(1, 0), stat(3, 0))
     m_both = jnp.maximum(m_near, m_away)
@@ -398,6 +424,19 @@
         merge(1, k)
         c_l[k].start()
 
+    span = 1024
+
+    def passage_grads(t):
+        cols = pl.ds(pl.multiple_of(t * span, span), span)
+        total = nn(wt_ref[...], qv[:, cols])
+        gp_ref[pl.ds(qd, pd - qd), cols] = (SCALE * total[qd:]).astype(BF16)
+        gp_ref[pl.ds(0, qd), cols] = (SCALE * (total[:qd] - qv[pl.ds(0, qd), cols].astype(F32))).astype(BF16)
+
+    loop(d // span, passage_grads)
+
+    request_sent()
+    answer_sent()
+
     top_l, top_r = jnp.maximum(m_l, m_x), jnp.maximum(m_r, m_x)
     factors[2, :, :] = jnp.broadcast_to(to_col(jnp.exp(jnp.where(front, top_l, m_l) - lse)), (qd, 128))
     factors[3, :, :] = jnp.broadcast_to(to_col(jnp.exp(jnp.where(front, m_r, top_r) - lse)), (qd, 128))
@@ -424,8 +463,6 @@
 
     for copy in [ag_r1, ag_r2, ag_r3, ag_l1, ag_l2, ag_l3] + b_r + b_l + c_r + c_l + st_copies + lse_copies:
         copy.wait_send()
-    request_sent()
-    answer_sent()
 
 
 def write_kernel(gp_in, gq_in, loss_in, gp_out, gq_out, loss_out, sems):
@@ -458,9 +495,12 @@
             pltpu.VMEM((qd, d), BF16),
             pltpu.VMEM((1, qd), F32),
         ),
-        in_specs=[any_spec] * 3 + [vmem_spec] * 3,
+        in_specs=[any_spec] * 6,
         out_specs=(vmem_spec, vmem_spec, vmem_spec),
         scratch_shapes=[
+            pltpu.VMEM(neg_ids.T.shape, I32),
+            pltpu.VMEM((1, qd), I32),
+            pltpu.VMEM((neg_home.shape[0] // 128, 128), I32),
             pltpu.VMEM((nx * qd, d), BF16),
             pltpu.VMEM((pd, d), BF16),
             pltpu.VMEM((n_rows, d), BF16),
@@ -486,7 +526,7 @@
             pltpu.VMEM((5, 8, qd), F32),
             pltpu.VMEM((8, qd), F32),
             pltpu.VMEM((3, 8, qd), F32),
-            dma((3,)),
+            dma((6,)),
             dma((6,)),
             dma((6,)),
             dma((4 + 4 * SUBS,)),
@@ -499,6 +539,8 @@
             dma((n_dp,)),
             dma((n_dp,)),
             dma((n_dp,)),
+            pltpu.SemaphoreType.REGULAR,
+            pltpu.SemaphoreType.REGULAR,
         ],
         compiler_params=pltpu.CompilerParams(
             collective_id=0, has_side_effects=True, vmem_limit_bytes=54 * 1024 * 1024

time: 91.8 us -> 82.1 us (0.89)
  Pallas kernels: 90.8 us -> 81.2 us
    pallas_call x1, Pallas kernels: 87.8 us -> 78.1 us  [per_device(): pl.pallas_call(functools.partial(exchange_kernel, n_dp), out_shape=(pltpu...]
where the time goes in v3:
time: 82.1 us; the launch traced here: 82 us
  Pallas kernels  81.2 us (99%)
    pallas_call x1, Pallas kernels, per_device(): pl.pallas_call(functools.partial(exchange_kernel, n_dp), out_shape=(pltpu...  78.1 us
    pallas_call x1, Pallas kernels, per_device(): pl.pallas_call(write_kernel, out_shape=(jax.ShapeDtypeStruct((pd, d), BF1...  3.05 us

profile of v3, /device:TPU:0, one launch (start us, length us, event | category | flops | bytes accessed | tf_op | source)
XLA Modules:
  0.0 82.0 jit_solution(16680992451566122464)
XLA Ops:
  0.6 78.1 %exchange.1 = (bf16[768,4096]{1,0:T(8,128)(2,1)S(1)}, bf16[128,4096]{1,0:T(8,128)(2,1)S(1)}, f32[1,128]{1,0:T(1,128)S(1)}) custom-call(bf16[128,4096]{1,0:T(8,128)(2,1)} %q_hbm.1, bf16[768,4096]{1,0:T(8,128)(2,1)} %p_hbm.1, bf16[1024,4096]{1,0:T(8,128)(2,1)} %t_hbm.1, s32[16,128]{1,0:T(8,128)} %bitcast.5, s32[1,128]{1,0:T(1,128)} %bitcast.6, s32[256,128]{1,0:T(8,128)} %bitcast.4), custom_call_target="tpu_custom_call" | custom-call | flops 12999999488 | bytes 25000000 | tf_op jit(solution)/shard_map/exchange/pallas_call | solution.py:491
  78.8 3.1 %write.1 = (bf16[768,4096]{1,0:T(8,128)(2,1)}, bf16[128,4096]{1,0:T(8,128)(2,1)}, f32[1,128]{1,0:T(1,128)}) custom-call(bf16[768,4096]{1,0:T(8,128)(2,1)S(1)} %get-tuple-element.9.gp_in, bf16[128,4096]{1,0:T(8,128)(2,1)S(1)} %get-tuple-element.10.gq_in, f32[1,128]{1,0:T(1,128)S(1)} %get-tuple-element.11.loss_in), custom_call_target="tpu_custom_call" | custom-call | bytes 7300000 | tf_op jit(solution)/shard_map/write/pallas_call | solution.py:551

commit v4 on v3

--- a/solution.py
+++ b/solution.py
@@ -193,11 +193,11 @@
             return remote(
                 out.at[pl.ds(pl.multiple_of(to * 16, 16), 16)],
                 inn.at[pl.ds(pl.multiple_of(frm * 16, 16), 16)],
-                send.at[j], recv.at[j], (to, me),
+                send.at[0], recv.at[0], (to, me),
             )
 
-        def came(j):
-            return copy(j, lax.rem(dp + n_dp - j, n_dp))
+        every = pl.ds(0, (n_dp - 1) * 16)
+        whole = remote(out.at[every], inn.at[every], send.at[0], recv.at[0], right)
 
         def begin():
             loop(n_dp - 1, lambda j: copy(j + 1, dp).start())
@@ -205,10 +205,10 @@
             inn[mine, :] = out[mine, :]
 
         def arrived():
-            loop(n_dp - 1, lambda j: came(j + 1).wait_recv())
+            whole.wait_recv()
 
         def sent():
-            loop(n_dp - 1, lambda j: came(j + 1).wait_send())
+            whole.wait_send()
 
         return begin, arrived, sent
 
@@ -219,21 +219,6 @@
     pack = [message_rows(n_msg, owner_row, c) for c in range(PIECES)]
     fill(req_out, pack, qv)
     req_out[:, piece:] = (nt(pack[0], meta_hi) + nt(pack[1], meta_lo)).astype(BF16)
-
-    @pl.when(me == 1)
-    def _():
-        pl.semaphore_wait(barrier, 2 * (n_dp - 1))
-        pl.semaphore_signal(peers_there, inc=1, device_id=(dp, 0), device_id_type=MESH)
-
-    @pl.when(me > 1)
-    def _():
-        pl.semaphore_wait(barrier, n_dp - 1)
-
-    @pl.when(first_plane)
-    def _():
-        pl.semaphore_wait(peers_there, 1)
-
-    request()
 
     def scores(block):
         cols = pl.ds(block * qd, qd)
@@ -258,6 +243,20 @@
     p_in.wait()
     scores(0)
     sums(base, 0)
+    @pl.when(me == 1)
+    def _():
+        pl.semaphore_wait(barrier, 2 * (n_dp - 1))
+        pl.semaphore_signal(peers_there, inc=1, device_id=(dp, 0), device_id_type=MESH)
+
+    @pl.when(me > 1)
+    def _():
+        pl.semaphore_wait(barrier, n_dp - 1)
+
+    @pl.when(first_plane)
+    def _():
+        pl.semaphore_wait(peers_there, 1)
+
+    request()
 
     ag_r1.wait_recv()
     ag_r3.start()
@@ -266,6 +265,24 @@
     scores(1)
     sums(ob, 0)
 
+    ag_r2.wait_recv()
+    ag_l2.wait_recv()
+    scores(2)
+    sums(ob, qd)
+
+    def back_step(i, block, part, k, n, dst, at, peer):
+        src = ob.at[half_rows(block - 1, part, k, n)]
+        return remote(src, dst.at[pl.ds(at, n)], rs_s.at[i], rs_r.at[i], peer)
+
+    both, quarter = 2, half // 2
+    b_r = [back_step(k, 1, 1, k * SUBS // 2, quarter, grecv.at[0], half + k * quarter, right) for k in range(both)]
+    b_l = [back_step(2 + k, 1, 0, k * SUBS // 2, quarter, grecv.at[1], k * quarter, left) for k in range(both)]
+    a_r = [back_step(4 + 4 * k, 3, 0, k, sub, arecv.at[0], k * sub, right) for k in range(SUBS)]
+    a_l = [back_step(5 + 4 * k, 3, 1, k, sub, arecv.at[1], k * sub, left) for k in range(SUBS)]
+    c_r = [back_step(6 + 4 * k, 2, 0, k, sub, grecv.at[0], k * sub, right) for k in range(SUBS)]
+    c_l = [back_step(7 + 4 * k, 2, 1, k, sub, grecv.at[1], half + k * sub, left) for k in range(SUBS)]
+    for copy in b_r + b_l:
+        copy.start()
     request_in()
     t_in.wait()
     asker = lax.shift_right_logical(iota((qd, 1), 0), 2)
@@ -314,24 +331,6 @@
     ret_out[:, piece:] = tail.astype(BF16)
     answer()
 
-    ag_r2.wait_recv()
-    ag_l2.wait_recv()
-    scores(2)
-    sums(ob, qd)
-
-    def back_step(i, block, part, k, n, dst, at, peer):
-        src = ob.at[half_rows(block - 1, part, k, n)]
-        return remote(src, dst.at[pl.ds(at, n)], rs_s.at[i], rs_r.at[i], peer)
-
-    both, quarter = 2, half // 2
-    b_r = [back_step(k, 1, 1, k * SUBS // 2, quarter, grecv.at[0], half + k * quarter, right) for k in range(both)]
-    b_l = [back_step(2 + k, 1, 0, k * SUBS // 2, quarter, grecv.at[1], k * quarter, left) for k in range(both)]
-    a_r = [back_step(4 + 4 * k, 3, 0, k, sub, arecv.at[0], k * sub, right) for k in range(SUBS)]
-    a_l = [back_step(5 + 4 * k, 3, 1, k, sub, arecv.at[1], k * sub, left) for k in range(SUBS)]
-    c_r = [back_step(6 + 4 * k, 2, 0, k, sub, grecv.at[0], k * sub, right) for k in range(SUBS)]
-    c_l = [back_step(7 + 4 * k, 2, 1, k, sub, grecv.at[1], half + k * sub, left) for k in range(SUBS)]
-    b_r[0].start()
-    b_l[0].start()
     ag_r3.wait_recv()
     ag_l3.wait_recv()
     scores(3)
@@ -385,14 +384,8 @@
         neg = nn(query_rows(n_msg, owner_col, c), ret_in[:, :piece])
         base[:, cols] = f_own * base[:, cols] + f_n * neg - pv[pl.ds(0, qd), cols].astype(F32)
 
-    for copy in lse_copies:
-        copy.wait_recv()
     front = iota((1, qd), 1) < half
-    lse_l, lse_r, lse_x = (lse_in[i, 0:1, :] for i in range(3))
-    by_block = (lse, jnp.where(front, lse_l, lse_r), jnp.where(front, lse_r, lse_l), lse_x)
-    for block in range(nx):
-        cols = pl.ds(block * qd, qd)
-        wt_ref[:, cols] = jnp.exp(s_ref[:, cols] - by_block[block]).astype(BF16)
+
     m_near = stats[2, 0:1, :]
     m_away = jnp.where(front, stat(1, 0), stat(3, 0))
     m_both = jnp.maximum(m_near, m_away)
@@ -411,11 +404,6 @@
 
         loop(d // 1024, body)
 
-    for k in range(SUBS):
-        a_r[k].wait_send()
-        a_l[k].wait_send()
-    b_r[1].start()
-    b_l[1].start()
     for k in range(SUBS):
         a_r[k].wait_recv()
         merge(0, k)
@@ -424,6 +412,13 @@
         merge(1, k)
         c_l[k].start()
 
+    for copy in lse_copies:
+        copy.wait_recv()
+    lse_l, lse_r, lse_x = (lse_in[i, 0:1, :] for i in range(3))
+    by_block = (lse, jnp.where(front, lse_l, lse_r), jnp.where(front, lse_r, lse_l), lse_x)
+    for block in range(nx):
+        cols = pl.ds(block * qd, qd)
+        wt_ref[:, cols] = jnp.exp(s_ref[:, cols] - by_block[block]).astype(BF16)
     span = 1024
 
     def passage_grads(t):
@@ -461,7 +456,7 @@
         c_l[k].wait_recv()
         finish(half + k * sub)
 
-    for copy in [ag_r1, ag_r2, ag_r3, ag_l1, ag_l2, ag_l3] + b_r + b_l + c_r + c_l + st_copies + lse_copies:
+    for copy in [ag_r1, ag_r2, ag_r3, ag_l1, ag_l2, ag_l3] + b_r + b_l + a_r + a_l + c_r + c_l + st_copies + lse_copies:
         copy.wait_send()
 
 
@@ -535,10 +530,10 @@
             dma((3,)),
             dma((3,)),
             dma((3,)),
-            dma((n_dp,)),
-            dma((n_dp,)),
-            dma((n_dp,)),
-            dma((n_dp,)),
+            dma((1,)),
+            dma((1,)),
+            dma((1,)),
+            dma((1,)),
             pltpu.SemaphoreType.REGULAR,
             pltpu.SemaphoreType.REGULAR,
         ],

time: 82.1 us -> 80 us (0.974)
  Pallas kernels: 81.2 us -> 79.1 us
    pallas_call x1, Pallas kernels: 78.1 us -> 76 us  [per_device(): pl.pallas_call(functools.partial(exchange_kernel, n_dp), out_shape=(pltpu...]
where the time goes in v4:
time: 80 us; the launch traced here: 79.9 us
  Pallas kernels  79.1 us (99%)
  between operations  0.8 us (1%)
    pallas_call x1, Pallas kernels, per_device(): pl.pallas_call(functools.partial(exchange_kernel, n_dp), out_shape=(pltpu...  76 us
    pallas_call x1, Pallas kernels, per_device(): pl.pallas_call(write_kernel, out_shape=(jax.ShapeDtypeStruct((pd, d), BF1...  3.05 us

profile of v4, /device:TPU:0, one launch (start us, length us, event | category | flops | bytes accessed | tf_op | source)
XLA Modules:
  0.0 79.9 jit_solution(7544494607757018711)
XLA Ops:
  0.6 76.0 %exchange.1 = (bf16[768,4096]{1,0:T(8,128)(2,1)S(1)}, bf16[128,4096]{1,0:T(8,128)(2,1)S(1)}, f32[1,128]{1,0:T(1,128)S(1)}) custom-call(bf16[128,4096]{1,0:T(8,128)(2,1)} %q_hbm.1, bf16[768,4096]{1,0:T(8,128)(2,1)} %p_hbm.1, bf16[1024,4096]{1,0:T(8,128)(2,1)} %t_hbm.1, s32[16,128]{1,0:T(8,128)} %bitcast.5, s32[1,128]{1,0:T(1,128)} %bitcast.6, s32[256,128]{1,0:T(8,128)} %bitcast.4), custom_call_target="tpu_custom_call" | custom-call | flops 12999999488 | bytes 25000000 | tf_op jit(solution)/shard_map/exchange/pallas_call | solution.py:486
  76.6 3.1 %write.1 = (bf16[768,4096]{1,0:T(8,128)(2,1)}, bf16[128,4096]{1,0:T(8,128)(2,1)}, f32[1,128]{1,0:T(1,128)}) custom-call(bf16[768,4096]{1,0:T(8,128)(2,1)S(1)} %get-tuple-element.9.gp_in, bf16[128,4096]{1,0:T(8,128)(2,1)S(1)} %get-tuple-element.10.gq_in, f32[1,128]{1,0:T(1,128)S(1)} %get-tuple-element.11.loss_in), custom_call_target="tpu_custom_call" | custom-call | bytes 7300000 | tf_op jit(solution)/shard_map/write/pallas_call | solution.py:546

commit v5 on v4

--- a/solution.py
+++ b/solution.py
@@ -12,7 +12,8 @@
 SCALE = 0.0625
 META = 128
 PIECES = 4
-SUBS = 4
+SUBS = 2
+HUB, AIDE = 2, 1
 
 
 def nn(a, b):
@@ -91,12 +92,11 @@
     across = (dp, lax.rem(me + 2, nx))
 
     barrier = pltpu.get_barrier_semaphore()
-    first_plane = me == 0
-    plane = jnp.maximum(me, 1)
-
-    @pl.when(me != 0)
+    plane = jnp.where(me == HUB, AIDE, me)
+
+    @pl.when(me != HUB)
     def _():
-        pl.semaphore_signal(barrier, inc=1, device_id=(dp, 0), device_id_type=MESH)
+        pl.semaphore_signal(barrier, inc=1, device_id=(dp, HUB), device_id_type=MESH)
 
     def greet(j):
         peer = lax.rem(dp + j + 1, n_dp)
@@ -116,13 +116,14 @@
     p_in.start()
     t_in.start()
 
-    @pl.when(first_plane)
+    @pl.when(me == HUB)
     def _():
         pl.semaphore_wait(barrier, nx - 1)
-        for b in range(1, nx):
-            pl.semaphore_signal(group_there, inc=1, device_id=(dp, b), device_id_type=MESH)
-
-    @pl.when(me != 0)
+        for b in range(nx):
+            if b != HUB:
+                pl.semaphore_signal(group_there, inc=1, device_id=(dp, b), device_id_type=MESH)
+
+    @pl.when(me != HUB)
     def _():
         pl.semaphore_wait(group_there, 1)
 
@@ -243,16 +244,16 @@
     p_in.wait()
     scores(0)
     sums(base, 0)
-    @pl.when(me == 1)
+    @pl.when(me == AIDE)
     def _():
         pl.semaphore_wait(barrier, 2 * (n_dp - 1))
-        pl.semaphore_signal(peers_there, inc=1, device_id=(dp, 0), device_id_type=MESH)
-
-    @pl.when(me > 1)
+        pl.semaphore_signal(peers_there, inc=1, device_id=(dp, HUB), device_id_type=MESH)
+
+    @pl.when((me != HUB) & (me != AIDE))
     def _():
         pl.semaphore_wait(barrier, n_dp - 1)
 
-    @pl.when(first_plane)
+    @pl.when(me == HUB)
     def _():
         pl.semaphore_wait(peers_there, 1)
 
@@ -274,13 +275,12 @@
         src = ob.at[half_rows(block - 1, part, k, n)]
         return remote(src, dst.at[pl.ds(at, n)], rs_s.at[i], rs_r.at[i], peer)
 
-    both, quarter = 2, half // 2
-    b_r = [back_step(k, 1, 1, k * SUBS // 2, quarter, grecv.at[0], half + k * quarter, right) for k in range(both)]
-    b_l = [back_step(2 + k, 1, 0, k * SUBS // 2, quarter, grecv.at[1], k * quarter, left) for k in range(both)]
-    a_r = [back_step(4 + 4 * k, 3, 0, k, sub, arecv.at[0], k * sub, right) for k in range(SUBS)]
-    a_l = [back_step(5 + 4 * k, 3, 1, k, sub, arecv.at[1], k * sub, left) for k in range(SUBS)]
-    c_r = [back_step(6 + 4 * k, 2, 0, k, sub, grecv.at[0], k * sub, right) for k in range(SUBS)]
-    c_l = [back_step(7 + 4 * k, 2, 1, k, sub, grecv.at[1], half + k * sub, left) for k in range(SUBS)]
+    b_r = [back_step(0, 1, 1, 0, half, grecv.at[0], half, right)]
+    b_l = [back_step(1, 1, 0, 0, half, grecv.at[1], 0, left)]
+    a_r = [back_step(2 + 4 * k, 3, 0, k, sub, arecv.at[0], k * sub, right) for k in range(SUBS)]
+    a_l = [back_step(3 + 4 * k, 3, 1, k, sub, arecv.at[1], k * sub, left) for k in range(SUBS)]
+    c_r = [back_step(4 + 4 * k, 2, 0, k, sub, grecv.at[0], k * sub, right) for k in range(SUBS)]
+    c_l = [back_step(5 + 4 * k, 2, 1, k, sub, grecv.at[1], half + k * sub, left) for k in range(SUBS)]
     for copy in b_r + b_l:
         copy.start()
     request_in()
@@ -524,8 +524,8 @@
             dma((6,)),
             dma((6,)),
             dma((6,)),
-            dma((4 + 4 * SUBS,)),
-            dma((4 + 4 * SUBS,)),
+            dma((2 + 4 * SUBS,)),
+            dma((2 + 4 * SUBS,)),
             dma((3,)),
             dma((3,)),
             dma((3,)),

time: 80 us -> 78.4 us (0.980)
  Pallas kernels: 79.1 us -> 77.5 us
    pallas_call x1, Pallas kernels: 76 us -> 74.5 us  [per_device(): pl.pallas_call(functools.partial(exchange_kernel, n_dp), out_shape=(pltpu...]
where the time goes in v5:
time: 78.4 us; the launch traced here: 78.3 us
  Pallas kernels  77.5 us (99%)
  between operations  0.8 us (1%)
    pallas_call x1, Pallas kernels, per_device(): pl.pallas_call(functools.partial(exchange_kernel, n_dp), out_shape=(pltpu...  74.5 us
    pallas_call x1, Pallas kernels, per_device(): pl.pallas_call(write_kernel, out_shape=(jax.ShapeDtypeStruct((pd, d), BF1...  3.05 us

profile of v5, /device:TPU:0, one launch (start us, length us, event | category | flops | bytes accessed | tf_op | source)
XLA Modules:
  0.0 78.3 jit_solution(13942994996828607598)
XLA Ops:
  0.6 74.5 %exchange.1 = (bf16[768,4096]{1,0:T(8,128)(2,1)S(1)}, bf16[128,4096]{1,0:T(8,128)(2,1)S(1)}, f32[1,128]{1,0:T(1,128)S(1)}) custom-call(bf16[128,4096]{1,0:T(8,128)(2,1)} %q_hbm.1, bf16[768,4096]{1,0:T(8,128)(2,1)} %p_hbm.1, bf16[1024,4096]{1,0:T(8,128)(2,1)} %t_hbm.1, s32[16,128]{1,0:T(8,128)} %bitcast.5, s32[1,128]{1,0:T(1,128)} %bitcast.6, s32[256,128]{1,0:T(8,128)} %bitcast.4), custom_call_target="tpu_custom_call" | custom-call | flops 12999999488 | bytes 25000000 | tf_op jit(solution)/shard_map/exchange/pallas_call | solution.py:486
  75.1 3.1 %write.1 = (bf16[768,4096]{1,0:T(8,128)(2,1)}, bf16[128,4096]{1,0:T(8,128)(2,1)}, f32[1,128]{1,0:T(1,128)}) custom-call(bf16[768,4096]{1,0:T(8,128)(2,1)S(1)} %get-tuple-element.9.gp_in, bf16[128,4096]{1,0:T(8,128)(2,1)S(1)} %get-tuple-element.10.gq_in, f32[1,128]{1,0:T(1,128)S(1)} %get-tuple-element.11.loss_in), custom_call_target="tpu_custom_call" | custom-call | bytes 7300000 | tf_op jit(solution)/shard_map/write/pallas_call | solution.py:546

commit v6 on v5

--- a/solution.py
+++ b/solution.py
@@ -440,23 +440,25 @@
         f_l, f_r = factors[2, pl.ds(at, sub), :1], factors[3, pl.ds(at, sub), :1]
 
         def body(t):
-            cols = pl.ds(pl.multiple_of(t * 1024, 1024), 1024)
+            cols = pl.ds(pl.multiple_of(t * 2048, 2048), 2048)
             total = base[pl.ds(at, sub), cols]
             total += f_l * grecv[0, pl.ds(at, sub), cols].astype(F32)
             total += f_r * grecv[1, pl.ds(at, sub), cols].astype(F32)
             gq_ref[pl.ds(at, sub), cols] = (SCALE * total).astype(BF16)
 
-        loop(d // 1024, body)
+        loop(d // 2048, body)
 
     for copy in b_r + b_l:
         copy.wait_recv()
+    for copy in [ag_r1, ag_r2, ag_r3, ag_l1, ag_l2, ag_l3] + b_r + b_l + a_r + a_l + st_copies + lse_copies:
+        copy.wait_send()
     for k in range(SUBS):
         c_r[k].wait_recv()
         finish(k * sub)
         c_l[k].wait_recv()
         finish(half + k * sub)
 
-    for copy in [ag_r1, ag_r2, ag_r3, ag_l1, ag_l2, ag_l3] + b_r + b_l + a_r + a_l + c_r + c_l + st_copies + lse_copies:
+    for copy in c_r + c_l:
         copy.wait_send()
 
 

time: 78.4 us -> 78.1 us (level)
  no operation moved by 1% of the time
where the time goes in v6:
time: 78.1 us; the launch traced here: 78 us
  Pallas kernels  77.2 us (99%)
  between operations  0.8 us (1%)
    pallas_call x1, Pallas kernels, per_device(): pl.pallas_call(functools.partial(exchange_kernel, n_dp), out_shape=(pltpu...  74.1 us
    pallas_call x1, Pallas kernels, per_device(): pl.pallas_call(write_kernel, out_shape=(jax.ShapeDtypeStruct((pd, d), BF1...  3.05 us

profile of v6, /device:TPU:0, one launch (start us, length us, event | category | flops | bytes accessed | tf_op | source)
XLA Modules:
  0.0 78.0 jit_solution(698417139888208585)
XLA Ops:
  0.6 74.1 %exchange.1 = (bf16[768,4096]{1,0:T(8,128)(2,1)S(1)}, bf16[128,4096]{1,0:T(8,128)(2,1)S(1)}, f32[1,128]{1,0:T(1,128)S(1)}) custom-call(bf16[128,4096]{1,0:T(8,128)(2,1)} %q_hbm.1, bf16[768,4096]{1,0:T(8,128)(2,1)} %p_hbm.1, bf16[1024,4096]{1,0:T(8,128)(2,1)} %t_hbm.1, s32[16,128]{1,0:T(8,128)} %bitcast.5, s32[1,128]{1,0:T(1,128)} %bitcast.6, s32[256,128]{1,0:T(8,128)} %bitcast.4), custom_call_target="tpu_custom_call" | custom-call | flops 12999999488 | bytes 25000000 | tf_op jit(solution)/shard_map/exchange/pallas_call | solution.py:488
  74.8 3.1 %write.1 = (bf16[768,4096]{1,0:T(8,128)(2,1)}, bf16[128,4096]{1,0:T(8,128)(2,1)}, f32[1,128]{1,0:T(1,128)}) custom-call(bf16[768,4096]{1,0:T(8,128)(2,1)S(1)} %get-tuple-element.9.gp_in, bf16[128,4096]{1,0:T(8,128)(2,1)S(1)} %get-tuple-element.10.gq_in, f32[1,128]{1,0:T(1,128)S(1)} %get-tuple-element.11.loss_in), custom_call_target="tpu_custom_call" | custom-call | bytes 7300000 | tf_op jit(solution)/shard_map/write/pallas_call | solution.py:548
